TPU v7x, 32 devices: a whole 2x2x4 slice. The times are simulated.
32 devices in a mesh: trace: 2 (over y), gx: 4 (over z), gy: 4 (over x, core).
Axes of the slice: x: 2, y: 2, z: 4, core: 2. Of those that a mesh axis runs over, the one named last changes fastest.
Arguments:
- traces: bfloat16 [8192, 4, 256], P(('trace', 'gx', 'gy')), may hold values from -4 to 4
- coupling: bfloat16 [8192, 4], P(('trace', 'gx', 'gy')), may hold values from 0.099609375 to 1.8984375
- tap_shift: int32 [8192], P(('trace', 'gx', 'gy')), may hold values from 0 to 63
- node_tile: int32 [8192, 1], P(('trace', 'gx', 'gy')), may hold values from 0 to 31; in each aligned block of 256 rows (0 to 255, 256 to 511, ...) at most 16 rows name the same one
- node_cell: int32 [8192], P(('trace', 'gx', 'gy')), may hold values from 0 to 524287
- field_prev: float32 [16, 1024, 1024], P('trace', 'gx', 'gy'), may hold values from -0.3125 to 0.3125
- field_now: float32 [16, 1024, 1024], P('trace', 'gx', 'gy'), may hold values from -0.3125 to 0.3125
- speed_sq: float32 [16, 1024, 1024], P('trace', 'gx', 'gy'), may hold values from 0.3 to 1
Outputs:
- out_prev: float32 [16, 1024, 1024], P('trace', 'gx', 'gy')
- out_now: float32 [16, 1024, 1024], P('trace', 'gx', 'gy')
Inputs may be any that keep to these rules, and one draw needn't show every extreme that they name: `node_tile`: among the nodes of one device at most 16 lie in one tile, and some device has exactly 16 in some tile.
All inputs are finite; a program needn't handle non-finite values.
Results may differ from a plain program's by a relative error of at most 0.0003.
Values may be sent and summed in bfloat16 or wider, within the bound.
No kernel may reach another device: no remote copies, remote signals or barrier semaphores. Data moves between devices by JAX's collectives and lax.ppermute only.
A program may use at most 128 MiB of HBM per device.

v0:
```python
import functools

import jax
import jax.numpy as jnp
import numpy as np
from jax import lax
from jax.experimental import pallas as pl
from jax.experimental.pallas import tpu as pltpu
from jax.sharding import PartitionSpec as P

NT = 256
STEPS = 4
RATE = 64
OFF = 16
GROUP = 16
SLOTS = 128
BATCH = 16
AXES = ("trace", "gx", "gy")
F32 = jnp.float32
BF16 = jnp.bfloat16
I32 = jnp.int32
I16 = jnp.int16
CODE_SCALES = (32767.0 / 0.3125, 32767.0 / 0.3125, 32767.0)
VMEM_LIMIT = 52 * 1024 * 1024
SMALL_LIMIT = 8 * 1024 * 1024


def log2(value):
    assert value & (value - 1) == 0
    return value.bit_length() - 1


def sinc_table():
    u = np.arange(NT)[None, :] + np.arange(STEPS * RATE)[:, None] - (NT - RATE // 2)
    u = u.astype(np.float64)
    table = np.sinc(u / RATE) * 0.5 * (1.0 + np.cos(np.pi * u / (2.0 * RATE)))
    return np.where(np.abs(u) < 2.0 * RATE, table, 0.0).astype(np.float32)


def vmem_spec():
    return pl.BlockSpec(memory_space=pltpu.VMEM)


def any_spec():
    return pl.BlockSpec(memory_space=pl.ANY)


def smem_spec():
    return pl.BlockSpec(memory_space=pltpu.SMEM)


def call(
    kernel, outs, in_specs, out_specs, scratch=(), bytes_accessed=0, flops=0, aliases=None,
    limit=VMEM_LIMIT
):
    return pl.pallas_call(
        kernel,
        out_shape=outs,
        in_specs=in_specs,
        out_specs=out_specs,
        scratch_shapes=list(scratch),
        input_output_aliases=aliases or {},
        compiler_params=pltpu.CompilerParams(vmem_limit_bytes=limit),
        cost_estimate=pl.CostEstimate(
            flops=flops, bytes_accessed=bytes_accessed, transcendentals=0
        ),
    )


def coded(values, field):
    return jnp.round(values * CODE_SCALES[field]).astype(I32).astype(I16)


def decoded(codes, field):
    return codes.astype(I32).astype(F32) * (1.0 / CODE_SCALES[field])


def in_hbm(*values):
    return [pltpu.with_memory_space_constraint(value, pltpu.HBM) for value in values]


def split3(values):
    first = values.astype(BF16).astype(F32)
    rest = values - first
    second = rest.astype(BF16).astype(F32)
    third = (rest - second).astype(BF16).astype(F32)
    return first, second, third


def amp_kernel(
    dims, traces_hbm, coupling_ref, ints_ref, table_hbm, out_ref,
    rank_ref, code_ref, count_ref, near_ref, traces_ref, table_ref, sems,
):
    nt, ngx, ngy, nz, nx, ny = dims
    count = nt * ngx * ngy
    nodes = traces_ref.shape[0]
    traces_copy = pltpu.make_async_copy(traces_hbm, traces_ref, sems.at[0])
    table_copy = pltpu.make_async_copy(table_hbm, table_ref, sems.at[1])
    traces_copy.start()
    table_copy.start()
    shift = ints_ref[0:1, :]
    tile = ints_ref[1:2, :]
    cell = ints_ref[2:3, :]
    gz = (tile >> log2(ngx * ngy)) * nz + (cell >> log2(nx * ny))
    gx = ((tile >> log2(ngy)) & (ngx - 1)) * nx + ((cell >> log2(ny)) & (nx - 1))
    gy = (tile & (ngy - 1)) * ny + (cell & (ny - 1))
    dest = lax.broadcasted_iota(I32, (count, nodes), 0)
    da = dest >> log2(ngx * ngy)
    lz = gz - da * nz
    lx = gx - ((dest >> log2(ngy)) & (ngx - 1)) * nx
    ly = gy - (dest & (ngy - 1)) * ny
    far = jnp.zeros((count, nodes), I32)
    for local, size in ((lz, nz), (lx, nx), (ly, ny)):
        far = far + jnp.maximum(-local, 0) + jnp.maximum(local - (size - 1), 0)
    held = far <= STEPS - 1
    plane = lz + da * (nz - 1 - 2 * lz) if nt == 2 else lz & 15
    code_ref[...] = ((plane << 18) + ((lx + OFF) << 9) + (ly + 8)).astype(F32)
    near = held & ((ly < 4) | (ly >= ny - 4))
    held_f = jnp.where(held, 1.0, 0.0)
    near_f = jnp.where(near, 1.0, 0.0)
    before = jnp.where(
        lax.broadcasted_iota(I32, (nodes, nodes), 0) < lax.broadcasted_iota(I32, (nodes, nodes), 1),
        1.0,
        0.0,
    )
    both = jnp.concatenate([held_f, near_f], axis=0).astype(BF16)
    rank = jnp.dot(both, before.astype(BF16), preferred_element_type=F32)
    rank, near_rank = rank[:count], rank[count:]
    counts = jnp.sum(held_f, axis=1, keepdims=True)
    nears = jnp.sum(near_f, axis=1, keepdims=True)
    rank = jnp.where(near, near_rank, nears + rank - near_rank)
    rank_ref[...] = jnp.where(held, rank, -1000.0)
    count_ref[...] = jnp.broadcast_to(counts, count_ref.shape)
    near_ref[...] = jnp.broadcast_to(nears, near_ref.shape)

    slot = lax.broadcasted_iota(I32, (SLOTS, nodes), 0).astype(F32)
    sub = lax.broadcasted_iota(I32, (8, nodes), 0)
    row = lax.broadcasted_iota(I32, (8, SLOTS), 0)
    traces_copy.wait()
    table_copy.wait()
    coupling = coupling_ref[...].astype(F32)
    combined = traces_ref[:, 0, :].astype(F32) * coupling[:, 0:1]
    for c in range(1, traces_ref.shape[1]):
        combined = combined + traces_ref[:, c, :].astype(F32) * coupling[:, c : c + 1]
    every = lax.dot_general(
        table_ref[...],
        combined,
        (((1,), (1,)), ((), ())),
        precision=lax.Precision.HIGHEST,
        preferred_element_type=F32,
    )
    tap = lax.broadcasted_iota(I32, every.shape, 0) & (RATE - 1)
    chosen = jnp.where(tap == shift, every, 0.0)
    amps = jnp.concatenate(
        [
            jnp.sum(chosen[s * RATE : (s + 1) * RATE], axis=0, keepdims=True)
            for s in range(STEPS)
        ],
        axis=0,
    )
    amp_parts = [jnp.concatenate([part, jnp.zeros_like(part)], axis=0) for part in split3(amps)]

    def tile_of(d, offset):
        hit = jnp.where(slot == rank_ref[pl.ds(d, 1), :] - offset, 1.0, 0.0)
        left = [
            jnp.where(sub == STEPS, code, part)
            for part, code in zip(amp_parts, split3(code_ref[pl.ds(d, 1), :]))
        ]
        got = lax.dot_general(
            jnp.concatenate(left, axis=0).astype(BF16),
            hit.astype(BF16),
            (((1,), (1,)), ((), ())),
            preferred_element_type=F32,
        )
        tile = jnp.where(row == STEPS + 1, count_ref[pl.ds(d, 1), :], got[0:8] + got[8:16] + got[16:24])
        return jnp.where(row == STEPS + 2, near_ref[pl.ds(d, 1), :], tile)

    out_ref[:, 8:, :] = jnp.zeros((count, out_ref.shape[1] - 8, SLOTS), F32)

    def first_tile(d, _):
        out_ref[d, 0:8, :] = tile_of(d, 0.0)
        return 0

    lax.fori_loop(0, count, first_tile, 0, unroll=8)

    @pl.when(jnp.max(counts) > SLOTS)
    def _():
        for r in range(1, out_ref.shape[1] // 8):

            def next_tile(d, _):
                out_ref[d, 8 * r : 8 * r + 8, :] = tile_of(d, r * float(SLOTS))
                return 0

            lax.fori_loop(0, count, next_tile, 0, unroll=8)


def z_entries(nz):
    return (
        [(0, g) for g in range(1, STEPS + 1)]
        + [(1, g) for g in range(1, STEPS)]
        + [(2, g) for g in range(1, STEPS)]
    )


def edge_entries():
    return (
        [(0, g) for g in range(1, STEPS)]
        + [(1, g) for g in range(1, STEPS - 1)]
        + [(2, g) for g in range(1, STEPS - 1)]
    )


def sides_of(nt):
    return ("hi",) if nt == 2 else ("hi", "lo")


def own_plane(nt, side, g, nz):
    return nz - g if nt == 2 or side == "lo" else g - 1


def ghost_plane(side, g, nz):
    return nz - 1 + g if side == "hi" else 16 - g


def flipped(plane, flip, nz):
    return plane + flip * (nz - 1 - 2 * plane)


def planes_kernel(nt, info_ref, now_ref, prev_ref, speed_ref, *rest):
    outs, (buffer, sems) = rest[:-2], rest[-2:]
    nz = now_ref.shape[0]
    flip = info_ref[0]
    copies = []
    for i, side in enumerate(sides_of(nt)):
        for k, (field, g) in enumerate(z_entries(nz)):
            source = (now_ref, prev_ref, speed_ref)[field]
            z = flipped(own_plane(nt, side, g, nz), flip, nz)
            at = i * len(z_entries(nz)) + k
            copy = pltpu.make_async_copy(source.at[z], buffer.at[at], sems.at[at])
            copy.start()
            copies.append((copy, i, k, at, field))
    for copy, i, k, at, field in copies:
        copy.wait()
        outs[i][k] = coded(buffer[at], field)


def packed(acc, base, tiles, source, lanes):
    for j, tile in enumerate(tiles):
        start = base + 4 * j
        moved = pltpu.roll(tile, lax.rem(start - source + 128, 128), 1)
        acc = jnp.where((lanes >= start) & (lanes < start + 4), moved, acc)
    return acc


def strips_kernel(
    info_ref, now_hbm, prev_hbm, speed_hbm, left_ref, right_ref, up_ref, down_ref, buffer, sems
):
    nz, nx, ny = now_hbm.shape
    flip = info_ref[0]
    copies = []
    for z in range(nz):
        for j, field in enumerate((now_hbm, prev_hbm, speed_hbm)):
            copy = pltpu.make_async_copy(field.at[z], buffer.at[j, z], sems.at[j, z])
            copy.start()
            copies.append(copy)
    left_ref[...] = jnp.zeros_like(left_ref)
    right_ref[...] = jnp.zeros_like(right_ref)
    rows = 64
    lanes = lax.broadcasted_iota(I32, (rows, 128), 1)
    low = lax.broadcasted_iota(I32, (8, ny), 0) < 4
    for z in range(nz):
        for copy in copies[3 * z : 3 * z + 3]:
            copy.wait()
        base = GROUP * flipped(z, flip, nz)
        for k in range(nx // rows):
            at = slice(k * rows, (k + 1) * rows)
            for ref, begin, source in ((left_ref, 0, 0), (right_ref, ny - 128, 124)):
                tiles = [buffer[j, z, at, begin : begin + 128] for j in range(3)]
                ref[at, :] = packed(ref[at, :], base, tiles, source, lanes)
        top, bottom = slice(nx - 8, nx), slice(0, 8)
        up_ref[0, z] = jnp.where(low, pltpu.roll(buffer[1, z, top, :], 4, 0), buffer[0, z, top, :])
        up_ref[1, z] = buffer[2, z, top, :]
        down_ref[0, z] = jnp.where(low, buffer[0, z, bottom, :], pltpu.roll(buffer[1, z, bottom, :], 4, 0))
        down_ref[1, z] = buffer[2, z, bottom, :]


def ghost_rows(ref, z, top):
    pair, speed = ref[0, z], ref[1, z]
    keep = lax.broadcasted_iota(I32, pair.shape, 0) < 4
    keep = jnp.logical_not(keep) if top else keep
    return (
        jnp.where(keep, pair, 0.0),
        jnp.where(keep, pltpu.roll(pair, 4, 0), 0.0),
        jnp.where(keep, speed, 0.0),
    )


def corners_kernel(info_ref, left_ref, right_ref, top_ref, bottom_ref, left_out, right_out):
    nx = left_ref.shape[0]
    nz, ny = top_ref.shape[1], top_ref.shape[3]
    lanes = lax.broadcasted_iota(I32, (8, 128), 1)
    for out, own, begin, source in ((left_out, left_ref, 0, 0), (right_out, right_ref, ny - 128, 124)):
        out[8 : 8 + nx, :] = own[...]
        for ref, top, row in ((top_ref, True, 0), (bottom_ref, False, 8 + nx)):
            acc = jnp.zeros((8, 128), F32)
            for z in range(nz):
                base = GROUP * flipped(z, info_ref[0], nz)
                tiles = [v[:, begin : begin + 128] for v in ghost_rows(ref, z, top)]
                acc = packed(acc, base, tiles, source, lanes)
            out[row : row + 8, :] = acc


def windows_kernel(nt, info_ref, left_ref, right_ref, from_left, from_right, top_ref, bottom_ref, own_ref, *outs):
    nz, ny = top_ref.shape[1], top_ref.shape[3]
    rows = left_ref.shape[0]
    step = 16
    lanes = lax.broadcasted_iota(I32, (step, 128), 1)
    inner = lanes & (GROUP - 1)

    def chunk(k, _):
        at = pl.ds(pl.multiple_of(k * step, step), step)
        parts = (from_left[at, :], left_ref[at, :], right_ref[at, :], from_right[at, :])
        windows = []
        for j in range(3):
            moved = [pltpu.roll(part, (4 * i - 4 * j) % 128, 1) for i, part in enumerate(parts)]
            window = jnp.where(
                inner < 4, moved[0], jnp.where(inner < 8, moved[1], jnp.where(inner < 12, moved[2], moved[3]))
            )
            own_ref[j, at, :] = window
            windows.append(window)
        for side, out in zip(sides_of(nt), outs):
            acc = jnp.zeros((step, 128), F32)
            for e, (field, g) in enumerate(edge_entries()):
                moved = pltpu.roll(windows[field], (GROUP * (e - own_plane(nt, side, g, nz))) % 128, 1)
                moved = moved * CODE_SCALES[field]
                acc = jnp.where((lanes >= GROUP * e) & (lanes < GROUP * (e + 1)), moved, acc)
            out[at, :] = jnp.round(acc).astype(I32).astype(I16)
        return 0

    lax.fori_loop(0, rows // step, chunk, 0, unroll=rows // step)
    for side, out in zip(sides_of(nt), outs):
        for e, (field, g) in enumerate(edge_entries()):
            z = flipped(own_plane(nt, side, g, nz), info_ref[0], nz)
            both = jnp.concatenate(
                [ghost_rows(top_ref, z, True)[field], ghost_rows(bottom_ref, z, False)[field]], axis=0
            )
            both = coded(both, field)
            for t in range(ny // 128):
                row = rows + (e * (ny // 128) + t) * 16
                out[row : row + 16, :] = both[:, t * 128 : (t + 1) * 128]


def sources_kernel(
    nt, info_ref, now_hbm, prev_hbm, speed_hbm, msg_hbm, top_ref, bottom_ref, own_ref, *rest
):
    a_ref, b_ref, c_ref, qa_ref, qb_ref, qc_ref, src, qsrc, load_sems, *node_scratch = rest
    nz, nx, ny = now_hbm.shape
    rows = nx + 2 * OFF
    lots = a_ref.shape[0] // rows
    flip = info_ref[0]

    erows = own_ref.shape[1]
    pltpu.make_async_copy(msg_hbm.at[:, pl.ds(0, 8), :], node_scratch[0], node_scratch[3].at[0]).start()
    loads = []
    for i, (field, ref) in enumerate(((now_hbm, a_ref), (prev_hbm, b_ref), (speed_hbm, c_ref))):
        for p in range(nz):
            copy = pltpu.make_async_copy(
                field.at[flipped(p, flip, nz)],
                ref.at[pl.ds(p * rows + OFF, nx), :],
                load_sems.at[i * nz + p],
            )
            copy.start()
            loads.append(copy)

    zero = jnp.zeros((rows, 128), F32)

    def clear_source(k, _):
        src[pl.ds(pl.multiple_of(k * rows, 8), rows), :] = zero
        return 0

    lax.fori_loop(0, src.shape[0] // rows, clear_source, 0)
    for k in range(qsrc.shape[0] // rows):
        qsrc[k * rows : (k + 1) * rows, :] = zero

    place_nodes = find_nodes(nx, ny, msg_hbm, src, qsrc, *node_scratch)
    edge_zero = jnp.zeros((16, ny), F32)
    for ref in (a_ref, b_ref, c_ref):
        for p in range(lots):
            ref[p * rows : p * rows + 16, :] = edge_zero
            ref[p * rows + OFF + nx : (p + 1) * rows, :] = edge_zero
    if nt == 2:
        for ref in (a_ref, b_ref):
            for t in range(ny // 128):
                ref[(lots - 1) * rows : lots * rows, t * 128 : (t + 1) * 128] = zero
    for p in range(nz):
        z = flipped(p, flip, nz)
        for ref, low, high in zip(
            (a_ref, b_ref, c_ref), ghost_rows(top_ref, z, True), ghost_rows(bottom_ref, z, False)
        ):
            ref[p * rows + 8 : p * rows + 16, :] = low
            ref[p * rows + OFF + nx : p * rows + OFF + nx + 8, :] = high
    for j, ref in enumerate((qa_ref, qb_ref, qc_ref)):
        ref[8 : 8 + erows, 0:128] = own_ref[j]
        ref[0:8, 0:128] = jnp.zeros((8, 128), F32)
        ref[8 + erows :, 0:128] = jnp.zeros((rows - 8 - erows, 128), F32)
        ref[:, 128:256] = zero
    place_nodes()
    for copy in loads:
        copy.wait()


def find_nodes(nx, ny, msg_hbm, src, qsrc, msg_ref, spots_ref, spots, in_sems):
    rows = nx + 2 * OFF
    flat = src.shape[0] // (2 * STEPS)
    senders = msg_hbm.shape[0]

    def first_row(at):
        return ((at >> 3) << 5) + (at & 7)

    def spot(word):
        return pl.ds(word >> 7, STEPS, stride=8)

    def msg_copy(r):
        return pltpu.make_async_copy(msg_hbm.at[:, pl.ds(8 * r, 8), :], msg_ref, in_sems.at[0])

    def spots_copy():
        return pltpu.make_async_copy(spots_ref, spots, in_sems.at[1])

    first_msg = msg_copy(0)
    def find_spots(whole):
        code = msg_ref[:, STEPS, :].astype(I32)
        p = code >> 18
        row = (code >> 9) & 511
        col = (code & 511) - 8
        index = lax.broadcasted_iota(I32, code.shape, 1)
        used = code != 0
        t = jnp.clip(col >> 7, 0, ny // 128 - 1)
        inside = used & (col >= 0) & (col < ny)
        spare = (index & 1) * flat + ((index >> 1) & 7)
        at = jnp.where(inside, t * flat + p * rows + row, spare)
        turn = (col - t * 128 - index) & 127
        clash = jnp.zeros(code.shape, I32)
        for j in range(1, BATCH):
            same = (at == pltpu.roll(at, j, 1)) & ((index & (BATCH - 1)) >= j) & (index < 2 * BATCH)
            clash = clash | jnp.where(same, 1, 0)
        word = (first_row(at) << 7) + turn
        spots_ref[0] = jnp.where(clash > 0, (first_row(spare) << 7) + turn, word)
        spots_ref[1] = word if whole else jnp.where((clash > 0) | (index >= 2 * BATCH), word, -1)
        low = col < 4
        qlane = GROUP * (p & 7) + jnp.where(low, col + 4, col - (ny - 4) + 8)
        spots_ref[2] = (first_row((p >> 3) * rows + row) << 7) + ((qlane - index) & 127)
        begin = jnp.where(jnp.max(clash, axis=1, keepdims=True) > 0, 0, 2 * BATCH)
        counts = msg_ref[:, STEPS + 1, :].astype(I32)
        nears = msg_ref[:, STEPS + 2, :].astype(I32)
        spots_ref[3] = jnp.where(index == 0, counts, jnp.where(index == 1, nears, begin))

    first_msg.wait()
    find_spots(False)
    spots_copy().start()
    lane = lax.broadcasted_iota(I32, (8, 128), 1)

    def share(d, k, turn):
        one = jnp.where(lane == k, msg_ref[d], 0.0)
        return pltpu.roll(one, turn, 1)[0:STEPS]

    def place_batch(d, first):
        words = [spots[0, d, k] for k in range(first, first + BATCH)]
        tile = msg_ref[d]
        values = [
            src[spot(word), :] + pltpu.roll(jnp.where(lane == first + k, tile, 0.0), word & 127, 1)[0:STEPS]
            for k, word in enumerate(words)
        ]
        for word, value in zip(words, values):
            src[spot(word), :] = value

    def place_first(d, _):
        place_batch(d, 0)
        return 0

    def place_second(i, _):
        group = [4 * i + j for j in range(4)]
        most = spots[3, group[0], 0]
        for d in group[1:]:
            most = jnp.maximum(most, spots[3, d, 0])

        @pl.when(most > BATCH)
        def _():
            for d in group:
                place_batch(d, BATCH)

        return 0

    def place_rest(r):
        def sender(d, most):
            count = spots[3, d, 0]

            def one(k, _):
                word = spots[1, d, k]

                @pl.when(word >= 0)
                def _():
                    src[spot(word), :] = src[spot(word), :] + share(d, k, word & 127)

                return 0

            def window(k, _):
                word = spots[2, d, k]
                qsrc[spot(word), :] = qsrc[spot(word), :] + share(d, k, word & 127)
                return 0

            first = 0 if r is not None else spots[3, d, 2]
            done = 0 if r is None else r * SLOTS
            lax.fori_loop(first, jnp.clip(count - done, 0, SLOTS), one, 0)
            lax.fori_loop(0, jnp.clip(spots[3, d, 1] - done, 0, SLOTS), window, 0)
            return jnp.maximum(most, count)

        return lax.fori_loop(0, senders, sender, 0)

    def place_nodes():
        spots_copy().wait()
        lax.fori_loop(0, senders, place_first, 0, unroll=4)
        lax.fori_loop(0, senders // 4, place_second, 0)
        most = place_rest(None)

        def extra(r, _):
            again = msg_copy(r)
            again.start()
            again.wait()
            find_spots(True)
            again = spots_copy()
            again.start()
            again.wait()
            place_rest(r)
            return 0

        lax.fori_loop(1, (most + SLOTS - 1) // SLOTS, extra, 0)

    return place_nodes


def steps_kernel(nt, info_ref, *rest):
    sides = sides_of(nt)
    n_side = len(sides)
    src, qsrc, rest = rest[6], rest[7], rest[8:]
    planes_in, rest = rest[:n_side], rest[n_side:]
    edges_in, rest = rest[:n_side], rest[n_side:]
    out_prev, out_now, a_ref, b_ref, c_ref, qa_ref, qb_ref, qc_ref, store_sems = rest
    nz, nx, ny = out_now.shape
    rows = nx + 2 * OFF
    lots = a_ref.shape[0] // rows
    flat = src.shape[0] // (2 * STEPS)
    erows = nx + 16
    flip = info_ref[0]
    for side, planes, edges in zip(sides, planes_in, edges_in):
        for k, (field, g) in enumerate(z_entries(nz)):
            ref = (a_ref, b_ref, c_ref)[field]
            at = ghost_plane(side, g, nz) * rows
            ref[at + OFF : at + OFF + nx, :] = decoded(planes[k], field)
        strip = edges[0:erows, :].astype(I32).astype(F32)
        lanes = lax.broadcasted_iota(I32, strip.shape, 1)
        for e, (field, g) in enumerate(edge_entries()):
            p = ghost_plane(side, g, nz)
            at = p * rows
            ref = (a_ref, b_ref, c_ref)[field]
            for t in range(ny // 128):
                row = erows + (e * (ny // 128) + t) * 16
                both = decoded(edges[row : row + 16, :], field)
                ref[at + 8 : at + 16, t * 128 : (t + 1) * 128] = both[0:8]
                ref[at + OFF + nx : at + OFF + nx + 8, t * 128 : (t + 1) * 128] = both[8:16]
            qref = (qa_ref, qb_ref, qc_ref)[field]
            lot = p - 8
            moved = pltpu.roll(strip, (GROUP * (lot - e)) % 128, 1) * (1.0 / CODE_SCALES[field])
            inside = (lanes >= GROUP * lot) & (lanes < GROUP * (lot + 1))
            qref[8 : 8 + erows, 128:256] = jnp.where(inside, moved, qref[8 : 8 + erows, 128:256])

    size = 16
    lanes = lax.broadcasted_iota(I32, (size, 128), 1)
    first, last = lanes == 0, lanes == 127

    def source_of(ref, at, s):
        return jnp.concatenate(
            [
                ref[pl.ds(pl.multiple_of((at + 8 * k) * STEPS + 8 * s, 8), 8), :]
                for k in range(size // 8)
            ],
            axis=0,
        )

    def main_step(s, now, prev, qnow, after=None):
        more = STEPS - 1 - s
        begin = OFF - 8 if more else OFF
        chunks = (nx + 16 if more else nx) // size

        def plane(i, _):
            p = i if nt == 2 else (i - more + lots) & (lots - 1)
            base = p * rows
            above = lax.rem(p + 1, lots) * rows
            below = lax.rem(p + lots - 1, lots) * rows
            qtile = pl.ds(pl.multiple_of((p >> 3) * 128, 128), 128)
            group = GROUP * (p & 7)
            to_first = lax.rem(256 - 3 - group, 128)
            to_last = lax.rem(256 + 127 - 12 - group, 128)

            def chunk(k, _):
                r0 = pl.multiple_of(begin + k * size, 8)

                def part(ref, at, t, extra=0):
                    at = pl.ds(pl.multiple_of(at + r0 - extra, 8), size + 2 * extra)
                    return ref[at, t * 128 : (t + 1) * 128]

                q = qnow[pl.ds(r0, size), qtile]
                mids = [part(now, base, t) for t in range(2)]
                ahead = [pltpu.roll(mid, 1, 1) for mid in mids]
                behind = [pltpu.roll(mid, 127, 1) for mid in mids]
                left = [
                    jnp.where(first, pltpu.roll(q, to_first, 1), ahead[0]),
                    jnp.where(first, ahead[0], ahead[1]),
                ]
                right = [
                    jnp.where(last, behind[1], behind[0]),
                    jnp.where(last, pltpu.roll(q, to_last, 1), behind[1]),
                ]
                for t in range(2):
                    wide = part(now, base, t, 8)
                    mid = mids[t]
                    beside = part(now, above, t) + part(now, below, t)
                    beside = beside + (wide[7 : 7 + size] + wide[9 : 9 + size])
                    beside = beside + (left[t] + right[t])
                    source = source_of(src, t * flat + base + r0, s)
                    result = (
                        2.0 * mid
                        - part(prev, base, t)
                        + (0.25 * part(c_ref, base, t)) * (beside - 6.0 * mid + source)
                    )
                    at = pl.ds(pl.multiple_of(base + r0, 8), size)
                    prev[at, t * 128 : (t + 1) * 128] = result
                return 0

            lax.fori_loop(0, chunks, chunk, 0, unroll=chunks)
            if after is not None:
                after(i)
            return 0

        lax.fori_loop(0, nz + n_side * more, plane, 0, unroll=True)

    def q_step(s, now, prev):
        def chunk(k, _):
            r0 = pl.multiple_of(OFF - 8 + k * size, 8)
            wide = now[pl.ds(pl.multiple_of(r0 - 8, 8), size + 16), :]
            mid = wide[8 : 8 + size]
            beside = wide[7 : 7 + size] + wide[9 : 9 + size]
            for shift in (1, 255, GROUP, 256 - GROUP):
                beside = beside + pltpu.roll(mid, shift, 1)
            at = pl.ds(r0, size)
            source = jnp.concatenate(
                [source_of(qsrc, r0, s), source_of(qsrc, rows + r0, s)], axis=1
            )
            prev[at, :] = (
                2.0 * mid
                - prev[at, :]
                + (0.25 * qc_ref[at, :]) * (beside - 6.0 * mid + source)
            )
            return 0

        lax.fori_loop(0, (nx + 16) // size, chunk, 0, unroll=(nx + 16) // size)

    fields, windows = [a_ref, b_ref], [qa_ref, qb_ref]

    def store(ref, out, p, sem):
        return pltpu.make_async_copy(
            ref.at[pl.ds(p * rows + OFF, nx), :], out.at[flipped(p, flip, nz)], sem
        )

    for s in range(STEPS - 1):
        main_step(s, fields[0], fields[1], windows[0])
        q_step(s, windows[0], windows[1])
        fields, windows = fields[::-1], windows[::-1]
    for p in range(nz):
        store(fields[0], out_prev, p, store_sems.at[p]).start()

    def finish(p):
        store(fields[1], out_now, p, store_sems.at[nz + p]).start()

    main_step(STEPS - 1, fields[0], fields[1], windows[0], finish)
    for p in range(nz):
        store(fields[0], out_prev, p, store_sems.at[p]).wait()
        store(fields[1], out_now, p, store_sems.at[nz + p]).wait()


def shifted(value, axis, count, step):
    pairs = [(i, i + step) for i in range(count) if 0 <= i + step < count]
    return lax.ppermute(value, axis, pairs)


def to_depth(values, nt):
    if nt == 2:
        return [lax.ppermute(values[0], "trace", [(0, 1), (1, 0)])]
    return [shifted(values[0], "trace", nt, -1), shifted(values[1], "trace", nt, 1)]


def body(traces, coupling, tap_shift, node_tile, node_cell, field_prev, field_now, speed_sq):
    nt, ngx, ngy = (lax.axis_size(axis) for axis in AXES)
    count = nt * ngx * ngy
    nodes = traces.shape[0]
    nz, nx, ny = field_now.shape
    sides = len(sides_of(nt))
    assert nz + 2 * STEPS == 16 and ny == 256
    shape = jax.ShapeDtypeStruct
    flip = lax.axis_index("trace") if nt == 2 else jnp.int32(0)
    info = jnp.full((1,), flip, I32)
    fields = (field_now, field_prev, speed_sq)

    entries = len(z_entries(nz))
    plane_msgs = call(
        functools.partial(planes_kernel, nt),
        [shape((entries, nx, ny), I16)] * sides,
        [smem_spec()] + [any_spec()] * 3,
        [vmem_spec()] * sides,
        [pltpu.VMEM((sides * entries, nx, ny), F32), pltpu.SemaphoreType.DMA((sides * entries,))],
        bytes_accessed=sides * entries * nx * ny * 6,
    )(info, *fields)
    planes = to_depth(plane_msgs, nt)

    left, right, up, down = call(
        strips_kernel,
        [shape((nx, 128), F32)] * 2 + [shape((2, nz, 8, ny), F32)] * 2,
        [smem_spec()] + [any_spec()] * 3,
        [vmem_spec()] * 4,
        [pltpu.VMEM((3, nz, nx, ny), F32), pltpu.SemaphoreType.DMA((3, nz))],
        bytes_accessed=3 * nz * nx * ny * 4,
    )(info, *fields)
    top = shifted(up, "gx", ngx, 1)
    bottom = shifted(down, "gx", ngx, -1)

    rounds = -(-nodes // SLOTS)
    ints = jnp.stack([tap_shift, node_tile[:, 0], node_cell])
    msg = call(
        functools.partial(amp_kernel, (nt, ngx, ngy, nz, nx, ny)),
        shape((count, 8 * rounds, SLOTS), F32),
        [any_spec(), vmem_spec(), vmem_spec(), any_spec()],
        vmem_spec(),
        [pltpu.VMEM((count, nodes), F32)] * 2
        + [pltpu.VMEM((count, SLOTS), F32)] * 2
        + [
            pltpu.VMEM(traces.shape, BF16),
            pltpu.VMEM((STEPS * RATE, NT), F32),
            pltpu.SemaphoreType.DMA((2,)),
        ],
        bytes_accessed=1 << 20,
        flops=1 << 30,
    )(*in_hbm(traces), coupling, ints, *in_hbm(jnp.asarray(sinc_table())))
    msg, top, bottom = lax.optimization_barrier((msg, top, bottom))
    msg = lax.all_to_all(msg, AXES, split_axis=0, concat_axis=0, tiled=True)

    erows = nx + 16
    left, right = call(
        corners_kernel,
        [shape((erows, 128), F32)] * 2,
        [smem_spec()] + [vmem_spec()] * 4,
        [vmem_spec()] * 2,
        bytes_accessed=1 << 20,
    )(info, left, right, top, bottom)
    from_left = shifted(right, "gy", ngy, 1)
    from_right = shifted(left, "gy", ngy, -1)

    edge_rows = erows + len(edge_entries()) * (ny // 128) * 16
    own, *edge_msgs = call(
        functools.partial(windows_kernel, nt),
        [shape((3, erows, 128), F32)] + [shape((edge_rows, 128), I16)] * sides,
        [smem_spec()] + [vmem_spec()] * 6,
        [vmem_spec()] * (1 + sides),
        bytes_accessed=1 << 20,
    )(info, left, right, from_left, from_right, top, bottom)
    edges = to_depth(edge_msgs, nt)

    rows = nx + 2 * OFF
    lots = nz + STEPS + 1 if nt == 2 else nz + 2 * STEPS
    source_lots = nz + STEPS - 1 if nt == 2 else lots
    state = [pltpu.VMEM((lots * rows, ny), F32)] * 3 + [pltpu.VMEM((rows, 256), F32)] * 3
    sources = [
        pltpu.VMEM((2 * source_lots * rows * STEPS, 128), F32),
        pltpu.VMEM((2 * rows * STEPS, 128), F32),
    ]
    held = call(
        functools.partial(sources_kernel, nt),
        state + sources,
        [smem_spec()] + [any_spec()] * 4 + [vmem_spec()] * 3,
        [vmem_spec()] * 8,
        [
            pltpu.SemaphoreType.DMA((3 * nz,)),
            pltpu.VMEM((count, 8, SLOTS), F32),
            pltpu.VMEM((4, count, SLOTS), I32),
            pltpu.SMEM((4, count, SLOTS), I32),
            pltpu.SemaphoreType.DMA((2,)),
        ],
        bytes_accessed=4 * nz * nx * ny * 4,
        flops=nz * nx * ny * 16,
        limit=SMALL_LIMIT,
    )(info, *in_hbm(*fields, msg), top, bottom, own)
    out_prev, out_now, *_ = call(
        functools.partial(steps_kernel, nt),
        [shape((nz, nx, ny), F32)] * 2 + state,
        [smem_spec()] + [vmem_spec()] * (8 + 2 * sides),
        [any_spec()] * 2 + [vmem_spec()] * 6,
        [pltpu.SemaphoreType.DMA((2 * nz,))],
        bytes_accessed=5 * nz * nx * ny * 4,
        flops=nz * nx * ny * STEPS * 16,
        aliases={1 + i: 2 + i for i in range(6)},
        limit=SMALL_LIMIT,
    )(info, *held, *planes, *edges)
    return out_prev, out_now


def solution(mesh):
    placed = (
        P(AXES, None, None),
        P(AXES, None),
        P(AXES),
        P(AXES, None),
        P(AXES),
        P("trace", "gx", "gy"),
        P("trace", "gx", "gy"),
        P("trace", "gx", "gy"),
    )
    return jax.shard_map(
        body,
        mesh=mesh,
        in_specs=placed,
        out_specs=(P("trace", "gx", "gy"), P("trace", "gx", "gy")),
        check_vma=False,
    )
```

profile of v0, /device:TPU:10, one launch (start us, length us, event | category | flops | bytes accessed | tf_op | source)
XLA Modules:
  0.0 58.9 jit_solution(15854487191089545866)
XLA Ops:
  0.6 1.8 %shard_map.109 = s16[10,256,256]{2,1,0:T(8,128)(2,1)S(1)} custom-call(s32[1]{0:T(128)} %bitcast.info_ref, f32[8,256,256]{2,1,0:T(8,128)} %now_ref.1, f32[8,256,256]{2,1,0:T(8,128)} %prev_ref.1, f32[8,256,256]{2,1,0:T(8,128)} %speed_ref.1), custom_call_target="tpu_custom_call" | custom-call | bytes 3932160 | tf_op jit(solution)/shard_map/pallas_call | solution.py:714
  2.4 0.0 copy-start.1
  2.4 0.0 copy-start.2
  2.4 0.0 copy-start.3
  2.5 0.0 copy-start
  2.5 1.6 %collective-permute-start.4 = (s16[10,256,256]{2,1,0:T(8,128)(2,1)S(1)}, s16[10,256,256]{2,1,0:T(8,128)(2,1)S(1)}, u32[]{:S(2)}, u32[]{:S(2)}) collective-permute-start(s16[10,256,256]{2,1,0:T(8,128)(2,1)S(1)} %shard_map.109), channel_id=1, source_target_pairs={{0,16},{16,0},{1,17},{17,1},{2,18},{18,2},{3,19},{19,3},{4,20},{20... | collective-permute-start | bytes 3932168 | tf_op jit(solution)/shard_map/ppermute | solution.py:697
  4.1 3.5 %shard_map.105 = (f32[256,128]{1,0:T(8,128)S(1)}, f32[256,128]{1,0:T(8,128)S(1)}, f32[2,8,8,256]{3,2,1,0:T(8,128)S(1)}, f32[2,8,8,256]{3,2,1,0:T(8,128)S(1)}) custom-call(s32[1]{0:T(128)} %bitcast.info_ref, f32[8,256,256]{2,1,0:T(8,128)} %now_ref.1, f32[8,256,256]{2,1,0:T(8,128)} %prev_ref.1, f32[8,256,256]{2,1,0:T(8,128)} %speed_ref.1), custom_call_target="tpu_custom_call" | custom-call | bytes 6291456 | tf_op jit(solution)/shard_map/pallas_call | solution.py:724
  7.6 3.5 %collective-permute-start = (f32[2,8,8,256]{3,2,1,0:T(8,128)S(1)}, f32[2,8,8,256]{3,2,1,0:T(8,128)S(1)}, u32[]{:S(2)}, u32[]{:S(2)}) collective-permute-start(f32[2,8,8,256]{3,2,1,0:T(8,128)S(1)} %get-tuple-element.23), channel_id=1, source_target_pairs={{0,4},{4,8},{8,12},{1,5},{5,9},{9,13},{2,6},{6,10},{10,14},{3,7},{... | collective-permute-start | bytes 393224 | tf_op jit(solution)/shard_map/ppermute | solution.py:692
  11.1 2.4 %collective-permute-start.1 = (f32[2,8,8,256]{3,2,1,0:T(8,128)S(1)}, f32[2,8,8,256]{3,2,1,0:T(8,128)S(1)}, u32[]{:S(2)}, u32[]{:S(2)}) collective-permute-start(f32[2,8,8,256]{3,2,1,0:T(8,128)S(1)} %get-tuple-element.24), channel_id=1, source_target_pairs={{4,0},{8,4},{12,8},{5,1},{9,5},{13,9},{6,2},{10,6},{14,10},{7,3},{... | collective-permute-start | bytes 393224 | tf_op jit(solution)/shard_map/ppermute | solution.py:692
  13.5 0.0 copy-done.1
  13.5 0.0 copy-done.2
  13.5 0.0 copy-done.3
  13.5 0.0 copy-done
  13.5 0.1 copy.17.coupling_ref
  13.7 3.9 %shard_map.104 = f32[32,16,128]{2,1,0:T(8,128)} custom-call(bf16[256,4,256]{2,1,0:T(4,128)(2,1)} %traces_hbm.1, bf16[256,4]{1,0:T(8,128)(2,1)S(1)} %copy.17.coupling_ref, s32[3,256]{1,0:T(4,128)S(1)} %pad_add_fusion.ints_ref, f32[256,256]{1,0:T(8,128)} %constant.8.clone.table_hbm), custom_call_target="tpu_custom_call" | custom-call | flops 1073741824 | bytes 1048576 | tf_op jit(solution)/shard_map/pallas_call | solution.py:737
  17.6 0.0 collective-permute-done.top_ref
  17.6 0.4 collective-permute-done.1.bottom_ref
  18.0 4.8 %all-to-all-start = ((f32[32,16,128]{2,1,0:T(8,128)}), f32[32,16,128]{2,1,0:T(8,128)}, u32[]{:S(2)}, u32[]{:S(2)}) async-start(f32[32,16,128]{2,1,0:T(8,128)} %shard_map.104), calls=%async_computation | async-start | bytes 524288 | tf_op jit(solution)/shard_map/all_to_all | solution.py:753
  22.7 0.2 shard_map.106
  23.0 2.2 %collective-permute-start.3 = (f32[272,128]{1,0:T(8,128)S(1)}, f32[272,128]{1,0:T(8,128)S(1)}, u32[]{:S(2)}, u32[]{:S(2)}) collective-permute-start(f32[272,128]{1,0:T(8,128)S(1)} %get-tuple-element.30.left_ref), channel_id=1, source_target_pairs={{1,0},{2,1},{3,2},{5,4},{6,5},{7,6},{9,8},{10,9},{11,10},{13,12},{... | collective-permute-start | bytes 417800 | tf_op jit(solution)/shard_map/ppermute | solution.py:692
  25.2 2.1 %collective-permute-start.2 = (f32[272,128]{1,0:T(8,128)S(1)}, f32[272,128]{1,0:T(8,128)S(1)}, u32[]{:S(2)}, u32[]{:S(2)}) collective-permute-start(f32[272,128]{1,0:T(8,128)S(1)} %get-tuple-element.31.right_ref), channel_id=1, source_target_pairs={{0,1},{1,2},{2,3},{4,5},{5,6},{6,7},{8,9},{9,10},{10,11},{12,13},{... | collective-permute-start | bytes 417800 | tf_op jit(solution)/shard_map/ppermute | solution.py:692
  27.3 1.2 %collective-permute-done.3.from_right = f32[272,128]{1,0:T(8,128)S(1)} collective-permute-done((f32[272,128]{1,0:T(8,128)S(1)}, f32[272,128]{1,0:T(8,128)S(1)}, u32[]{:S(2)}, u32[]{:S(2)}) %collective-permute-start.3) | collective-permute-done | bytes 139296 | tf_op jit(solution)/shard_map/ppermute | solution.py:692
  28.5 3.3 %collective-permute-done.2.from_left = f32[272,128]{1,0:T(8,128)S(1)} collective-permute-done((f32[272,128]{1,0:T(8,128)S(1)}, f32[272,128]{1,0:T(8,128)S(1)}, u32[]{:S(2)}, u32[]{:S(2)}) %collective-permute-start.2) | collective-permute-done | bytes 139296 | tf_op jit(solution)/shard_map/ppermute | solution.py:692
  31.7 1.4 %shard_map.107 = (f32[3,272,128]{2,1,0:T(8,128)S(1)}, s16[496,128]{1,0:T(8,128)(2,1)S(1)}) custom-call(s32[1]{0:T(128)} %bitcast.info_ref, f32[272,128]{1,0:T(8,128)S(1)} %get-tuple-element.30.left_ref, f32[272,128]{1,0:T(8,128)S(1)} %get-tuple-element.31.right_ref, f32[272,128]{1,0:T(8,128)S(1)} %collective-permute-done.2.from_left, ...), custom_call_target="tpu_custom_call" | custom-call | bytes 1048576 | tf_op jit(solution)/shard_map/pallas_call | solution.py:767
  33.1 1.5 %collective-permute-start.5 = (s16[496,128]{1,0:T(8,128)(2,1)S(1)}, s16[496,128]{1,0:T(8,128)(2,1)S(1)}, u32[]{:S(2)}, u32[]{:S(2)}) collective-permute-start(s16[496,128]{1,0:T(8,128)(2,1)S(1)} %get-tuple-element.41), channel_id=1, source_target_pairs={{0,16},{16,0},{1,17},{17,1},{2,18},{18,2},{3,19},{19,3},{4,20},{20... | collective-permute-start | bytes 380936 | tf_op jit(solution)/shard_map/ppermute | solution.py:697
  34.6 2.5 %all-to-all-done.msg_hbm = f32[32,16,128]{2,1,0:T(8,128)} async-done(((f32[32,16,128]{2,1,0:T(8,128)}), f32[32,16,128]{2,1,0:T(8,128)}, u32[]{:S(2)}, u32[]{:S(2)}) %all-to-all-start) | async-done | bytes 262176 | tf_op jit(solution)/shard_map/all_to_all | solution.py:753
  37.1 10.7 %shard_map.108 = (f32[3744,256]{1,0:T(8,128)S(1)}, f32[3744,256]{1,0:T(8,128)S(1)}, f32[3744,256]{1,0:T(8,128)S(1)}, f32[288,256]{1,0:T(8,128)S(1)}, f32[288,256...) custom-call(s32[1]{0:T(128)} %bitcast.info_ref, ...), custom_call_target="tpu_custom_call" | custom-call | flops 8388608 | bytes 8388608 | tf_op jit(solution)/shard_map/pallas_call | solution.py:784
  47.9 0.0 collective-permute-done.5.rest_9_
  47.9 0.0 collective-permute-done.4.rest_8_
  47.9 10.8 %shard_map.110 = (f32[8,256,256]{2,1,0:T(8,128)}, f32[8,256,256]{2,1,0:T(8,128)}, f32[3744,256]{1,0:T(8,128)S(1)}, f32[3744,256]{1,0:T(8,128)S(1)}, f32[3744,256...) custom-call(s32[1]{0:T(128)} %bitcast.info_ref, ...), custom_call_target="tpu_custom_call", output_to_operand_aliasing={{2}: (1, {}), {3}: (2, {}), {4}: (3, {}), {5}: (4, {}), {6}... | custom-call | flops 33554432 | bytes 10485760 | tf_op jit(solution)/shard_map/pallas_call | solution.py:800
  (1 shorter events, 0.0 us)
Async XLA Ops:
  2.4 11.0 %copy-start.1 = (s32[256]{0:T(256)S(1)}, s32[256]{0:T(256)}, u32[]{:S(2)}) copy-start(s32[256]{0:T(256)} %param.13) | copy-start | bytes 3076
  2.4 11.0 %copy-start.2 = (s32[256,1]{0,1:T(1,128)S(1)}, s32[256,1]{0,1:T(1,128)}, u32[]{:S(2)}) copy-start(s32[256,1]{0,1:T(1,128)} %param.12) | copy-start | bytes 3076
  2.4 11.0 %copy-start.3 = (s32[256]{0:T(256)S(1)}, s32[256]{0:T(256)}, u32[]{:S(2)}) copy-start(s32[256]{0:T(256)} %param.11) | copy-start | bytes 3076
  2.5 11.1 %copy-start = (bf16[256,4]{0,1:T(4,128)(2,1)S(1)}, bf16[256,4]{0,1:T(4,128)(2,1)}, u32[]{:S(2)}) copy-start(bf16[256,4]{0,1:T(4,128)(2,1)} %param.10) | copy-start | bytes 6148
  2.5 45.4 %collective-permute-start.4 = (s16[10,256,256]{2,1,0:T(8,128)(2,1)S(1)}, s16[10,256,256]{2,1,0:T(8,128)(2,1)S(1)}, u32[]{:S(2)}, u32[]{:S(2)}) collective-permute-start(s16[10,256,256]{2,1,0:T(8,128)(2,1)S(1)} %shard_map.109), channel_id=1, source_target_pairs={{0,16},{16,0},{1,17},{17,1},{2,18},{18,2},{3,19},{19,3},{4,20},{20... | collective-permute-start | bytes 3932168 | tf_op jit(solution)/shard_map/ppermute | solution.py:697
  7.6 10.0 %collective-permute-start = (f32[2,8,8,256]{3,2,1,0:T(8,128)S(1)}, f32[2,8,8,256]{3,2,1,0:T(8,128)S(1)}, u32[]{:S(2)}, u32[]{:S(2)}) collective-permute-start(f32[2,8,8,256]{3,2,1,0:T(8,128)S(1)} %get-tuple-element.23), channel_id=1, source_target_pairs={{0,4},{4,8},{8,12},{1,5},{5,9},{9,13},{2,6},{6,10},{10,14},{3,7},{... | collective-permute-start | bytes 393224 | tf_op jit(solution)/shard_map/ppermute | solution.py:692
  11.1 6.9 %collective-permute-start.1 = (f32[2,8,8,256]{3,2,1,0:T(8,128)S(1)}, f32[2,8,8,256]{3,2,1,0:T(8,128)S(1)}, u32[]{:S(2)}, u32[]{:S(2)}) collective-permute-start(f32[2,8,8,256]{3,2,1,0:T(8,128)S(1)} %get-tuple-element.24), channel_id=1, source_target_pairs={{4,0},{8,4},{12,8},{5,1},{9,5},{13,9},{6,2},{10,6},{14,10},{7,3},{... | collective-permute-start | bytes 393224 | tf_op jit(solution)/shard_map/ppermute | solution.py:692
  18.0 19.2 %all-to-all-start = ((f32[32,16,128]{2,1,0:T(8,128)}), f32[32,16,128]{2,1,0:T(8,128)}, u32[]{:S(2)}, u32[]{:S(2)}) async-start(f32[32,16,128]{2,1,0:T(8,128)} %shard_map.104), calls=%async_computation | async-start | bytes 524288 | tf_op jit(solution)/shard_map/all_to_all | solution.py:753
  23.0 5.5 %collective-permute-start.3 = (f32[272,128]{1,0:T(8,128)S(1)}, f32[272,128]{1,0:T(8,128)S(1)}, u32[]{:S(2)}, u32[]{:S(2)}) collective-permute-start(f32[272,128]{1,0:T(8,128)S(1)} %get-tuple-element.30.left_ref), channel_id=1, source_target_pairs={{1,0},{2,1},{3,2},{5,4},{6,5},{7,6},{9,8},{10,9},{11,10},{13,12},{... | collective-permute-start | bytes 417800 | tf_op jit(solution)/shard_map/ppermute | solution.py:692
  25.2 6.5 %collective-permute-start.2 = (f32[272,128]{1,0:T(8,128)S(1)}, f32[272,128]{1,0:T(8,128)S(1)}, u32[]{:S(2)}, u32[]{:S(2)}) collective-permute-start(f32[272,128]{1,0:T(8,128)S(1)} %get-tuple-element.31.right_ref), channel_id=1, source_target_pairs={{0,1},{1,2},{2,3},{4,5},{5,6},{6,7},{8,9},{9,10},{10,11},{12,13},{... | collective-permute-start | bytes 417800 | tf_op jit(solution)/shard_map/ppermute | solution.py:692
  33.1 14.8 %collective-permute-start.5 = (s16[496,128]{1,0:T(8,128)(2,1)S(1)}, s16[496,128]{1,0:T(8,128)(2,1)S(1)}, u32[]{:S(2)}, u32[]{:S(2)}) collective-permute-start(s16[496,128]{1,0:T(8,128)(2,1)S(1)} %get-tuple-element.41), channel_id=1, source_target_pairs={{0,16},{16,0},{1,17},{17,1},{2,18},{18,2},{3,19},{19,3},{4,20},{20... | collective-permute-start | bytes 380936 | tf_op jit(solution)/shard_map/ppermute | solution.py:697
where the time goes:
time: 58.9 us
  Pallas kernels  32.4 us (55%)
  starting transfers between devices  18.1 us (31%)
  waiting for transfers between devices  7.27 us (12%)
  between operations  0.98 us (2%)
    pallas_call x1, Pallas kernels, body(): call(functools.partial(steps_kernel, nt), [shape((nz, nx, ny), F32)] * 2...  10.8 us
    pallas_call x1, Pallas kernels, body(): call(functools.partial(sources_kernel, nt), state + sources, [smem_spec()...  10.7 us
    ppermute x4, starting transfers between devices, shifted(): return lax.ppermute(value, axis, pairs)  10.2 us
    ppermute x4, waiting for transfers between devices, shifted(): return lax.ppermute(value, axis, pairs)  4.79 us
    all_to_all x1, starting transfers between devices, body(): msg = lax.all_to_all(msg, AXES, split_axis=0, concat_axis=0, tiled=True)  4.78 us
    pallas_call x1, Pallas kernels, body(): call(functools.partial(amp_kernel, (nt, ngx, ngy, nz, nx, ny)), shape((co...  3.92 us
    pallas_call x1, Pallas kernels, body(): call(strips_kernel, [shape((nx, 128), F32)] * 2 + [shape((2, nz, 8, ny),...  3.54 us
    ppermute x2, starting transfers between devices, to_depth(): return [lax.ppermute(values[0], 'trace', [(0, 1), (1, 0)])]  3.12 us
  transfers between devices with their start and end apart: 7, of which 4 were waited for; matrix products, arithmetic and copies ran while one was open for 0% of the time, Pallas kernels for 34%

commit v1 on v0

--- a/solution.py
+++ b/solution.py
@@ -14,6 +14,7 @@
 OFF = 16
 GROUP = 16
 SLOTS = 128
+EARLY = 8
 BATCH = 16
 AXES = ("trace", "gx", "gy")
 F32 = jnp.float32
@@ -241,7 +242,8 @@
             copies.append((copy, i, k, at, field))
     for copy, i, k, at, field in copies:
         copy.wait()
-        outs[i][k] = coded(buffer[at], field)
+        out, first = (outs[2 * i], 0) if k < EARLY else (outs[2 * i + 1], EARLY)
+        out[k - first] = coded(buffer[at], field)
 
 
 def packed(acc, base, tiles, source, lanes):
@@ -252,8 +254,39 @@
     return acc
 
 
-def strips_kernel(
-    info_ref, now_hbm, prev_hbm, speed_hbm, left_ref, right_ref, up_ref, down_ref, buffer, sems
+def rows_kernel(now_hbm, prev_hbm, speed_hbm, up_ref, down_ref, buffer, sems):
+    nz, nx, ny = now_hbm.shape
+    copies = []
+    for j, field in enumerate((now_hbm, prev_hbm, speed_hbm)):
+        for i, begin in enumerate((nx - 8, 0)):
+            copy = pltpu.make_async_copy(
+                field.at[:, pl.ds(begin, 8), :], buffer.at[j, i], sems.at[j, i]
+            )
+            copy.start()
+            copies.append(copy)
+    for copy in copies:
+        copy.wait()
+    low = lax.broadcasted_iota(I32, (8, ny), 0) < 4
+    for z in range(nz):
+        up_ref[0, z] = jnp.where(low, pltpu.roll(buffer[1, 0, z], 4, 0), buffer[0, 0, z])
+        up_ref[1, z] = buffer[2, 0, z]
+        down_ref[0, z] = jnp.where(low, buffer[0, 1, z], pltpu.roll(buffer[1, 1, z], 4, 0))
+        down_ref[1, z] = buffer[2, 1, z]
+
+
+def ghost_rows(ref, z, top):
+    pair, speed = ref[0, z], ref[1, z]
+    keep = lax.broadcasted_iota(I32, pair.shape, 0) < 4
+    keep = jnp.logical_not(keep) if top else keep
+    return (
+        jnp.where(keep, pair, 0.0),
+        jnp.where(keep, pltpu.roll(pair, 4, 0), 0.0),
+        jnp.where(keep, speed, 0.0),
+    )
+
+
+def columns_kernel(
+    info_ref, now_hbm, prev_hbm, speed_hbm, top_ref, bottom_ref, left_ref, right_ref, buffer, sems
 ):
     nz, nx, ny = now_hbm.shape
     flip = info_ref[0]
@@ -263,51 +296,29 @@
             copy = pltpu.make_async_copy(field.at[z], buffer.at[j, z], sems.at[j, z])
             copy.start()
             copies.append(copy)
-    left_ref[...] = jnp.zeros_like(left_ref)
-    right_ref[...] = jnp.zeros_like(right_ref)
+    sides = ((left_ref, 0, 0), (right_ref, ny - 128, 124))
+    lanes = lax.broadcasted_iota(I32, (8, 128), 1)
+    for out, begin, source in sides:
+        for ref, top, row in ((top_ref, True, 0), (bottom_ref, False, 8 + nx)):
+            acc = jnp.zeros((8, 128), F32)
+            for z in range(nz):
+                base = GROUP * flipped(z, flip, nz)
+                tiles = [v[:, begin : begin + 128] for v in ghost_rows(ref, z, top)]
+                acc = packed(acc, base, tiles, source, lanes)
+            out[row : row + 8, :] = acc
+        out[8 : 8 + nx, :] = jnp.zeros((nx, 128), F32)
     rows = 64
     lanes = lax.broadcasted_iota(I32, (rows, 128), 1)
-    low = lax.broadcasted_iota(I32, (8, ny), 0) < 4
     for z in range(nz):
         for copy in copies[3 * z : 3 * z + 3]:
             copy.wait()
         base = GROUP * flipped(z, flip, nz)
         for k in range(nx // rows):
             at = slice(k * rows, (k + 1) * rows)
-            for ref, begin, source in ((left_ref, 0, 0), (right_ref, ny - 128, 124)):
+            to = slice(8 + k * rows, 8 + (k + 1) * rows)
+            for ref, begin, source in sides:
                 tiles = [buffer[j, z, at, begin : begin + 128] for j in range(3)]
-                ref[at, :] = packed(ref[at, :], base, tiles, source, lanes)
-        top, bottom = slice(nx - 8, nx), slice(0, 8)
-        up_ref[0, z] = jnp.where(low, pltpu.roll(buffer[1, z, top, :], 4, 0), buffer[0, z, top, :])
-        up_ref[1, z] = buffer[2, z, top, :]
-        down_ref[0, z] = jnp.where(low, buffer[0, z, bottom, :], pltpu.roll(buffer[1, z, bottom, :], 4, 0))
-        down_ref[1, z] = buffer[2, z, bottom, :]
-
-
-def ghost_rows(ref, z, top):
-    pair, speed = ref[0, z], ref[1, z]
-    keep = lax.broadcasted_iota(I32, pair.shape, 0) < 4
-    keep = jnp.logical_not(keep) if top else keep
-    return (
-        jnp.where(keep, pair, 0.0),
-        jnp.where(keep, pltpu.roll(pair, 4, 0), 0.0),
-        jnp.where(keep, speed, 0.0),
-    )
-
-
-def corners_kernel(info_ref, left_ref, right_ref, top_ref, bottom_ref, left_out, right_out):
-    nx = left_ref.shape[0]
-    nz, ny = top_ref.shape[1], top_ref.shape[3]
-    lanes = lax.broadcasted_iota(I32, (8, 128), 1)
-    for out, own, begin, source in ((left_out, left_ref, 0, 0), (right_out, right_ref, ny - 128, 124)):
-        out[8 : 8 + nx, :] = own[...]
-        for ref, top, row in ((top_ref, True, 0), (bottom_ref, False, 8 + nx)):
-            acc = jnp.zeros((8, 128), F32)
-            for z in range(nz):
-                base = GROUP * flipped(z, info_ref[0], nz)
-                tiles = [v[:, begin : begin + 128] for v in ghost_rows(ref, z, top)]
-                acc = packed(acc, base, tiles, source, lanes)
-            out[row : row + 8, :] = acc
+                ref[to, :] = packed(ref[to, :], base, tiles, source, lanes)
 
 
 def windows_kernel(nt, info_ref, left_ref, right_ref, from_left, from_right, top_ref, bottom_ref, own_ref, *outs):
@@ -373,16 +384,6 @@
             loads.append(copy)
 
     zero = jnp.zeros((rows, 128), F32)
-
-    def clear_source(k, _):
-        src[pl.ds(pl.multiple_of(k * rows, 8), rows), :] = zero
-        return 0
-
-    lax.fori_loop(0, src.shape[0] // rows, clear_source, 0)
-    for k in range(qsrc.shape[0] // rows):
-        qsrc[k * rows : (k + 1) * rows, :] = zero
-
-    place_nodes = find_nodes(nx, ny, msg_hbm, src, qsrc, *node_scratch)
     edge_zero = jnp.zeros((16, ny), F32)
     for ref in (a_ref, b_ref, c_ref):
         for p in range(lots):
@@ -404,6 +405,15 @@
         ref[0:8, 0:128] = jnp.zeros((8, 128), F32)
         ref[8 + erows :, 0:128] = jnp.zeros((rows - 8 - erows, 128), F32)
         ref[:, 128:256] = zero
+    place_nodes = find_nodes(nx, ny, msg_hbm, src, qsrc, *node_scratch)
+
+    def clear_source(k, _):
+        src[pl.ds(pl.multiple_of(k * rows, 8), rows), :] = zero
+        return 0
+
+    lax.fori_loop(0, src.shape[0] // rows, clear_source, 0)
+    for k in range(qsrc.shape[0] // rows):
+        qsrc[k * rows : (k + 1) * rows, :] = zero
     place_nodes()
     for copy in loads:
         copy.wait()
@@ -543,6 +553,7 @@
     n_side = len(sides)
     src, qsrc, rest = rest[6], rest[7], rest[8:]
     planes_in, rest = rest[:n_side], rest[n_side:]
+    later_in, rest = rest[:n_side], rest[n_side:]
     edges_in, rest = rest[:n_side], rest[n_side:]
     out_prev, out_now, a_ref, b_ref, c_ref, qa_ref, qb_ref, qc_ref, store_sems = rest
     nz, nx, ny = out_now.shape
@@ -551,11 +562,11 @@
     flat = src.shape[0] // (2 * STEPS)
     erows = nx + 16
     flip = info_ref[0]
-    for side, planes, edges in zip(sides, planes_in, edges_in):
+    for side, planes, later, edges in zip(sides, planes_in, later_in, edges_in):
         for k, (field, g) in enumerate(z_entries(nz)):
             ref = (a_ref, b_ref, c_ref)[field]
             at = ghost_plane(side, g, nz) * rows
-            ref[at + OFF : at + OFF + nx, :] = decoded(planes[k], field)
+            ref[at + OFF : at + OFF + nx, :] = decoded(planes[k] if k < EARLY else later[k - EARLY], field)
         strip = edges[0:erows, :].astype(I32).astype(F32)
         lanes = lax.broadcasted_iota(I32, strip.shape, 1)
         for e, (field, g) in enumerate(edge_entries()):
@@ -713,22 +724,22 @@
     entries = len(z_entries(nz))
     plane_msgs = call(
         functools.partial(planes_kernel, nt),
-        [shape((entries, nx, ny), I16)] * sides,
+        [shape((EARLY, nx, ny), I16), shape((entries - EARLY, nx, ny), I16)] * sides,
         [smem_spec()] + [any_spec()] * 3,
-        [vmem_spec()] * sides,
+        [vmem_spec()] * (2 * sides),
         [pltpu.VMEM((sides * entries, nx, ny), F32), pltpu.SemaphoreType.DMA((sides * entries,))],
         bytes_accessed=sides * entries * nx * ny * 6,
     )(info, *fields)
-    planes = to_depth(plane_msgs, nt)
-
-    left, right, up, down = call(
-        strips_kernel,
-        [shape((nx, 128), F32)] * 2 + [shape((2, nz, 8, ny), F32)] * 2,
-        [smem_spec()] + [any_spec()] * 3,
-        [vmem_spec()] * 4,
-        [pltpu.VMEM((3, nz, nx, ny), F32), pltpu.SemaphoreType.DMA((3, nz))],
-        bytes_accessed=3 * nz * nx * ny * 4,
-    )(info, *fields)
+    planes = to_depth(plane_msgs[0::2], nt)
+
+    up, down = call(
+        rows_kernel,
+        [shape((2, nz, 8, ny), F32)] * 2,
+        [any_spec()] * 3,
+        [vmem_spec()] * 2,
+        [pltpu.VMEM((3, 2, nz, 8, ny), F32), pltpu.SemaphoreType.DMA((3, 2))],
+        bytes_accessed=1 << 20,
+    )(*fields)
     top = shifted(up, "gx", ngx, 1)
     bottom = shifted(down, "gx", ngx, -1)
 
@@ -754,14 +765,19 @@
 
     erows = nx + 16
     left, right = call(
-        corners_kernel,
+        columns_kernel,
         [shape((erows, 128), F32)] * 2,
-        [smem_spec()] + [vmem_spec()] * 4,
+        [smem_spec()] + [any_spec()] * 3 + [vmem_spec()] * 2,
         [vmem_spec()] * 2,
-        bytes_accessed=1 << 20,
-    )(info, left, right, top, bottom)
+        [pltpu.VMEM((3, nz, nx, ny), F32), pltpu.SemaphoreType.DMA((3, nz))],
+        bytes_accessed=3 * nz * nx * ny * 4,
+    )(info, *fields, top, bottom)
     from_left = shifted(right, "gy", ngy, 1)
     from_right = shifted(left, "gy", ngy, -1)
+    from_left, from_right, *later = lax.optimization_barrier(
+        (from_left, from_right, *plane_msgs[1::2])
+    )
+    later = to_depth(later, nt)
 
     edge_rows = erows + len(edge_entries()) * (ny // 128) * 16
     own, *edge_msgs = call(
@@ -800,14 +816,14 @@
     out_prev, out_now, *_ = call(
         functools.partial(steps_kernel, nt),
         [shape((nz, nx, ny), F32)] * 2 + state,
-        [smem_spec()] + [vmem_spec()] * (8 + 2 * sides),
+        [smem_spec()] + [vmem_spec()] * (8 + 3 * sides),
         [any_spec()] * 2 + [vmem_spec()] * 6,
         [pltpu.SemaphoreType.DMA((2 * nz,))],
         bytes_accessed=5 * nz * nx * ny * 4,
         flops=nz * nx * ny * STEPS * 16,
         aliases={1 + i: 2 + i for i in range(6)},
         limit=SMALL_LIMIT,
-    )(info, *held, *planes, *edges)
+    )(info, *held, *planes, *later, *edges)
     return out_prev, out_now
 
 

time: 58.9 us -> 56.7 us (0.963)
  the two profiles are of different devices: /device:TPU:10 before, /device:TPU:25 now
where the time goes in v1:
time: 56.7 us; the launch traced here: 55.9 us
  Pallas kernels  32.9 us (58%)
  starting transfers between devices  19.8 us (35%)
  waiting for transfers between devices  2.02 us (4%)
  between operations  0.99 us (2%)
    ppermute x4, starting transfers between devices, shifted(): return lax.ppermute(value, axis, pairs)  10.8 us
    pallas_call x1, Pallas kernels, body(): call(functools.partial(steps_kernel, nt), [shape((nz, nx, ny), F32)] * 2...  10.8 us
    pallas_call x1, Pallas kernels, body(): call(functools.partial(sources_kernel, nt), state + sources, [smem_spec()...  10.2 us
    all_to_all x1, starting transfers between devices, body(): msg = lax.all_to_all(msg, AXES, split_axis=0, concat_axis=0, tiled=True)  6.13 us
    pallas_call x1, Pallas kernels, body(): call(functools.partial(amp_kernel, (nt, ngx, ngy, nz, nx, ny)), shape((co...  3.92 us
    pallas_call x1, Pallas kernels, body(): call(columns_kernel, [shape((erows, 128), F32)] * 2, [smem_spec()] + [any...  3.67 us
    ppermute x3, starting transfers between devices, to_depth(): return [lax.ppermute(values[0], 'trace', [(0, 1), (1, 0)])]  2.83 us
    ppermute x4, waiting for transfers between devices, shifted(): return lax.ppermute(value, axis, pairs)  2.01 us
  transfers between devices with their start and end apart: 8, of which 2 were waited for; matrix products, arithmetic and copies ran while one was open for 0% of the time, Pallas kernels for 36%

profile of v1, /device:TPU:25, one launch (start us, length us, event | category | flops | bytes accessed | tf_op | source)
XLA Modules:
  0.0 55.9 jit_solution(1314630978684925995)
XLA Ops:
  0.6 1.8 %shard_map.107 = (s16[8,256,256]{2,1,0:T(8,128)(2,1)S(1)}, s16[2,256,256]{2,1,0:T(8,128)(2,1)S(1)}) custom-call(s32[1]{0:T(128)} %bitcast.info_ref, f32[8,256,256]{2,1,0:T(8,128)} %now_hbm.5, f32[8,256,256]{2,1,0:T(8,128)} %prev_hbm.5, f32[8,256,256]{2,1,0:T(8,128)} %speed_hbm.5), custom_call_target="tpu_custom_call" | custom-call | bytes 3932160 | tf_op jit(solution)/shard_map/pallas_call | solution.py:725
  2.4 0.0 copy-start.1
  2.4 0.0 copy-start.2
  2.4 0.0 copy-start.3
  2.5 0.0 copy-start
  2.5 1.3 %collective-permute-start.4 = (s16[8,256,256]{2,1,0:T(8,128)(2,1)S(1)}, s16[8,256,256]{2,1,0:T(8,128)(2,1)S(1)}, u32[]{:S(2)}, u32[]{:S(2)}) collective-permute-start(s16[8,256,256]{2,1,0:T(8,128)(2,1)S(1)} %get-tuple-element.45), channel_id=1, source_target_pairs={{0,16},{16,0},{1,17},{17,1},{2,18},{18,2},{3,19},{19,3},{4,20},{20... | collective-permute-start | bytes 3145736 | tf_op jit(solution)/shard_map/ppermute | solution.py:708
  3.8 1.1 %shard_map.105 = (f32[2,8,8,256]{3,2,1,0:T(8,128)S(1)}, f32[2,8,8,256]{3,2,1,0:T(8,128)S(1)}) custom-call(f32[8,256,256]{2,1,0:T(8,128)} %now_hbm.5, f32[8,256,256]{2,1,0:T(8,128)} %prev_hbm.5, f32[8,256,256]{2,1,0:T(8,128)} %speed_hbm.5), custom_call_target="tpu_custom_call" | custom-call | bytes 1048576 | tf_op jit(solution)/shard_map/pallas_call | solution.py:735
  4.9 1.3 %collective-permute-start = (f32[2,8,8,256]{3,2,1,0:T(8,128)S(1)}, f32[2,8,8,256]{3,2,1,0:T(8,128)S(1)}, u32[]{:S(2)}, u32[]{:S(2)}) collective-permute-start(f32[2,8,8,256]{3,2,1,0:T(8,128)S(1)} %get-tuple-element.26), channel_id=1, source_target_pairs={{0,4},{4,8},{8,12},{1,5},{5,9},{9,13},{2,6},{6,10},{10,14},{3,7},{... | collective-permute-start | bytes 393224 | tf_op jit(solution)/shard_map/ppermute | solution.py:703
  6.2 4.0 %collective-permute-start.1 = (f32[2,8,8,256]{3,2,1,0:T(8,128)S(1)}, f32[2,8,8,256]{3,2,1,0:T(8,128)S(1)}, u32[]{:S(2)}, u32[]{:S(2)}) collective-permute-start(f32[2,8,8,256]{3,2,1,0:T(8,128)S(1)} %get-tuple-element.27), channel_id=1, source_target_pairs={{4,0},{8,4},{12,8},{5,1},{9,5},{13,9},{6,2},{10,6},{14,10},{7,3},{... | collective-permute-start | bytes 393224 | tf_op jit(solution)/shard_map/ppermute | solution.py:703
  10.2 0.0 copy-done.1
  10.2 0.0 copy-done.2
  10.2 0.0 copy-done.3
  10.2 0.0 copy-done
  10.2 0.1 copy.17.coupling_ref
  10.4 3.9 %shard_map.104 = f32[32,16,128]{2,1,0:T(8,128)} custom-call(bf16[256,4,256]{2,1,0:T(4,128)(2,1)} %traces_hbm.1, bf16[256,4]{1,0:T(8,128)(2,1)S(1)} %copy.17.coupling_ref, s32[3,256]{1,0:T(4,128)S(1)} %pad_add_fusion.ints_ref, f32[256,256]{1,0:T(8,128)} %constant.8.clone.table_hbm), custom_call_target="tpu_custom_call" | custom-call | flops 1073741824 | bytes 1048576 | tf_op jit(solution)/shard_map/pallas_call | solution.py:748
  14.3 0.0 collective-permute-done.top_ref
  14.3 0.0 collective-permute-done.1.bottom_ref
  14.3 6.1 %all-to-all-start = ((f32[32,16,128]{2,1,0:T(8,128)}), f32[32,16,128]{2,1,0:T(8,128)}, u32[]{:S(2)}, u32[]{:S(2)}) async-start(f32[32,16,128]{2,1,0:T(8,128)} %shard_map.104), calls=%async_computation | async-start | bytes 524288 | tf_op jit(solution)/shard_map/all_to_all | solution.py:764
  20.4 3.7 %shard_map.106 = (f32[272,128]{1,0:T(8,128)S(1)}, f32[272,128]{1,0:T(8,128)S(1)}) custom-call(s32[1]{0:T(128)} %bitcast.info_ref, f32[8,256,256]{2,1,0:T(8,128)} %now_hbm.5, f32[8,256,256]{2,1,0:T(8,128)} %prev_hbm.5, f32[8,256,256]{2,1,0:T(8,128)} %speed_hbm.5, f32[2,8,8,256]{3,2,1,0:T(8,128)S(1)} %collective-permute-done.top_ref, ...), custom_call_target="tpu_custom_call" | custom-call | bytes 6291456 | tf_op jit(solution)/shard_map/pallas_call | solution.py:767
  24.1 2.3 %collective-permute-start.3 = (f32[272,128]{1,0:T(8,128)S(1)}, f32[272,128]{1,0:T(8,128)S(1)}, u32[]{:S(2)}, u32[]{:S(2)}) collective-permute-start(f32[272,128]{1,0:T(8,128)S(1)} %get-tuple-element.31.left_ref), channel_id=1, source_target_pairs={{1,0},{2,1},{3,2},{5,4},{6,5},{7,6},{9,8},{10,9},{11,10},{13,12},{... | collective-permute-start | bytes 417800 | tf_op jit(solution)/shard_map/ppermute | solution.py:703
  26.4 3.3 %collective-permute-start.2 = (f32[272,128]{1,0:T(8,128)S(1)}, f32[272,128]{1,0:T(8,128)S(1)}, u32[]{:S(2)}, u32[]{:S(2)}) collective-permute-start(f32[272,128]{1,0:T(8,128)S(1)} %get-tuple-element.32.right_ref), channel_id=1, source_target_pairs={{0,1},{1,2},{2,3},{4,5},{5,6},{6,7},{8,9},{9,10},{10,11},{12,13},{... | collective-permute-start | bytes 417800 | tf_op jit(solution)/shard_map/ppermute | solution.py:703
  29.7 0.9 %collective-permute-done.3.from_right = f32[272,128]{1,0:T(8,128)S(1)} collective-permute-done((f32[272,128]{1,0:T(8,128)S(1)}, f32[272,128]{1,0:T(8,128)S(1)}, u32[]{:S(2)}, u32[]{:S(2)}) %collective-permute-start.3) | collective-permute-done | bytes 139296 | tf_op jit(solution)/shard_map/ppermute | solution.py:703
  30.6 1.1 %collective-permute-done.2.from_left = f32[272,128]{1,0:T(8,128)S(1)} collective-permute-done((f32[272,128]{1,0:T(8,128)S(1)}, f32[272,128]{1,0:T(8,128)S(1)}, u32[]{:S(2)}, u32[]{:S(2)}) %collective-permute-start.2) | collective-permute-done | bytes 139296 | tf_op jit(solution)/shard_map/ppermute | solution.py:703
  31.7 1.2 %collective-permute-start.5 = (s16[2,256,256]{2,1,0:T(8,128)(2,1)S(1)}, s16[2,256,256]{2,1,0:T(8,128)(2,1)S(1)}, u32[]{:S(2)}, u32[]{:S(2)}) collective-permute-start(s16[2,256,256]{2,1,0:T(8,128)(2,1)S(1)} %get-tuple-element.46), channel_id=1, source_target_pairs={{0,16},{16,0},{1,17},{17,1},{2,18},{18,2},{3,19},{19,3},{4,20},{20... | collective-permute-start | bytes 786440 | tf_op jit(solution)/shard_map/ppermute | solution.py:708
  32.9 1.4 %shard_map.108 = (f32[3,272,128]{2,1,0:T(8,128)S(1)}, s16[496,128]{1,0:T(8,128)(2,1)S(1)}) custom-call(s32[1]{0:T(128)} %bitcast.info_ref, f32[272,128]{1,0:T(8,128)S(1)} %get-tuple-element.31.left_ref, f32[272,128]{1,0:T(8,128)S(1)} %get-tuple-element.32.right_ref, f32[272,128]{1,0:T(8,128)S(1)} %collective-permute-done.2.from_left, ...), custom_call_target="tpu_custom_call" | custom-call | bytes 1048576 | tf_op jit(solution)/shard_map/pallas_call | solution.py:783
  34.3 0.3 collective-permute-start.6
  34.6 0.0 all-to-all-done.msg_hbm
  34.6 10.2 %shard_map.109 = (f32[3744,256]{1,0:T(8,128)S(1)}, f32[3744,256]{1,0:T(8,128)S(1)}, f32[3744,256]{1,0:T(8,128)S(1)}, f32[288,256]{1,0:T(8,128)S(1)}, f32[288,256...) custom-call(s32[1]{0:T(128)} %bitcast.info_ref, ...), custom_call_target="tpu_custom_call" | custom-call | flops 8388608 | bytes 8388608 | tf_op jit(solution)/shard_map/pallas_call | solution.py:800
  44.8 0.0 collective-permute-done.6.rest_10_
  44.8 0.0 collective-permute-done.5.rest_9_
  44.8 0.0 collective-permute-done.4.rest_8_
  44.9 10.8 %shard_map.110 = (f32[8,256,256]{2,1,0:T(8,128)}, f32[8,256,256]{2,1,0:T(8,128)}, f32[3744,256]{1,0:T(8,128)S(1)}, f32[3744,256]{1,0:T(8,128)S(1)}, f32[3744,256...) custom-call(s32[1]{0:T(128)} %bitcast.info_ref, ...), custom_call_target="tpu_custom_call", output_to_operand_aliasing={{2}: (1, {}), {3}: (2, {}), {4}: (3, {}), {5}: (4, {}), {6}... | custom-call | flops 33554432 | bytes 10485760 | tf_op jit(solution)/shard_map/pallas_call | solution.py:816
  (1 shorter events, 0.0 us)
Async XLA Ops:
  2.4 7.7 %copy-start.1 = (s32[256]{0:T(256)S(1)}, s32[256]{0:T(256)}, u32[]{:S(2)}) copy-start(s32[256]{0:T(256)} %param.13) | copy-start | bytes 3076
  2.4 7.7 %copy-start.2 = (s32[256,1]{0,1:T(1,128)S(1)}, s32[256,1]{0,1:T(1,128)}, u32[]{:S(2)}) copy-start(s32[256,1]{0,1:T(1,128)} %param.12) | copy-start | bytes 3076
  2.4 7.7 %copy-start.3 = (s32[256]{0:T(256)S(1)}, s32[256]{0:T(256)}, u32[]{:S(2)}) copy-start(s32[256]{0:T(256)} %param.11) | copy-start | bytes 3076
  2.5 7.7 %copy-start = (bf16[256,4]{0,1:T(4,128)(2,1)S(1)}, bf16[256,4]{0,1:T(4,128)(2,1)}, u32[]{:S(2)}) copy-start(bf16[256,4]{0,1:T(4,128)(2,1)} %param.10) | copy-start | bytes 6148
  2.5 42.4 %collective-permute-start.4 = (s16[8,256,256]{2,1,0:T(8,128)(2,1)S(1)}, s16[8,256,256]{2,1,0:T(8,128)(2,1)S(1)}, u32[]{:S(2)}, u32[]{:S(2)}) collective-permute-start(s16[8,256,256]{2,1,0:T(8,128)(2,1)S(1)} %get-tuple-element.45), channel_id=1, source_target_pairs={{0,16},{16,0},{1,17},{17,1},{2,18},{18,2},{3,19},{19,3},{4,20},{20... | collective-permute-start | bytes 3145736 | tf_op jit(solution)/shard_map/ppermute | solution.py:708
  4.9 9.4 %collective-permute-start = (f32[2,8,8,256]{3,2,1,0:T(8,128)S(1)}, f32[2,8,8,256]{3,2,1,0:T(8,128)S(1)}, u32[]{:S(2)}, u32[]{:S(2)}) collective-permute-start(f32[2,8,8,256]{3,2,1,0:T(8,128)S(1)} %get-tuple-element.26), channel_id=1, source_target_pairs={{0,4},{4,8},{8,12},{1,5},{5,9},{9,13},{2,6},{6,10},{10,14},{3,7},{... | collective-permute-start | bytes 393224 | tf_op jit(solution)/shard_map/ppermute | solution.py:703
  6.2 8.1 %collective-permute-start.1 = (f32[2,8,8,256]{3,2,1,0:T(8,128)S(1)}, f32[2,8,8,256]{3,2,1,0:T(8,128)S(1)}, u32[]{:S(2)}, u32[]{:S(2)}) collective-permute-start(f32[2,8,8,256]{3,2,1,0:T(8,128)S(1)} %get-tuple-element.27), channel_id=1, source_target_pairs={{4,0},{8,4},{12,8},{5,1},{9,5},{13,9},{6,2},{10,6},{14,10},{7,3},{... | collective-permute-start | bytes 393224 | tf_op jit(solution)/shard_map/ppermute | solution.py:703
  14.3 20.3 %all-to-all-start = ((f32[32,16,128]{2,1,0:T(8,128)}), f32[32,16,128]{2,1,0:T(8,128)}, u32[]{:S(2)}, u32[]{:S(2)}) async-start(f32[32,16,128]{2,1,0:T(8,128)} %shard_map.104), calls=%async_computation | async-start | bytes 524288 | tf_op jit(solution)/shard_map/all_to_all | solution.py:764
  24.1 6.5 %collective-permute-start.3 = (f32[272,128]{1,0:T(8,128)S(1)}, f32[272,128]{1,0:T(8,128)S(1)}, u32[]{:S(2)}, u32[]{:S(2)}) collective-permute-start(f32[272,128]{1,0:T(8,128)S(1)} %get-tuple-element.31.left_ref), channel_id=1, source_target_pairs={{1,0},{2,1},{3,2},{5,4},{6,5},{7,6},{9,8},{10,9},{11,10},{13,12},{... | collective-permute-start | bytes 417800 | tf_op jit(solution)/shard_map/ppermute | solution.py:703
  26.4 5.3 %collective-permute-start.2 = (f32[272,128]{1,0:T(8,128)S(1)}, f32[272,128]{1,0:T(8,128)S(1)}, u32[]{:S(2)}, u32[]{:S(2)}) collective-permute-start(f32[272,128]{1,0:T(8,128)S(1)} %get-tuple-element.32.right_ref), channel_id=1, source_target_pairs={{0,1},{1,2},{2,3},{4,5},{5,6},{6,7},{8,9},{9,10},{10,11},{12,13},{... | collective-permute-start | bytes 417800 | tf_op jit(solution)/shard_map/ppermute | solution.py:703
  31.7 13.1 %collective-permute-start.5 = (s16[2,256,256]{2,1,0:T(8,128)(2,1)S(1)}, s16[2,256,256]{2,1,0:T(8,128)(2,1)S(1)}, u32[]{:S(2)}, u32[]{:S(2)}) collective-permute-start(s16[2,256,256]{2,1,0:T(8,128)(2,1)S(1)} %get-tuple-element.46), channel_id=1, source_target_pairs={{0,16},{16,0},{1,17},{17,1},{2,18},{18,2},{3,19},{19,3},{4,20},{20... | collective-permute-start | bytes 786440 | tf_op jit(solution)/shard_map/ppermute | solution.py:708
  34.3 10.5 %collective-permute-start.6 = (s16[496,128]{1,0:T(8,128)(2,1)S(1)}, s16[496,128]{1,0:T(8,128)(2,1)S(1)}, u32[]{:S(2)}, u32[]{:S(2)}) collective-permute-start(s16[496,128]{1,0:T(8,128)(2,1)S(1)} %get-tuple-element.47), channel_id=1, source_target_pairs={{0,16},{16,0},{1,17},{17,1},{2,18},{18,2},{3,19},{19,3},{4,20},{20... | collective-permute-start | bytes 380936 | tf_op jit(solution)/shard_map/ppermute | solution.py:708

commit v2 on v1

--- a/solution.py
+++ b/solution.py
@@ -528,7 +528,7 @@
 
     def place_nodes():
         spots_copy().wait()
-        lax.fori_loop(0, senders, place_first, 0, unroll=4)
+        lax.fori_loop(0, senders, place_first, 0, unroll=8)
         lax.fori_loop(0, senders // 4, place_second, 0)
         most = place_rest(None)
 
@@ -760,7 +760,7 @@
         bytes_accessed=1 << 20,
         flops=1 << 30,
     )(*in_hbm(traces), coupling, ints, *in_hbm(jnp.asarray(sinc_table())))
-    msg, top, bottom = lax.optimization_barrier((msg, top, bottom))
+    msg, top = lax.optimization_barrier((msg, top))
     msg = lax.all_to_all(msg, AXES, split_axis=0, concat_axis=0, tiled=True)
 
     erows = nx + 16

time: 56.7 us -> 57.2 us (level)
  the two profiles are of different devices: /device:TPU:25 before, /device:TPU:10 now
where the time goes in v2:
time: 57.2 us; the launch traced here: 56.9 us
  Pallas kernels  32.4 us (57%)
  starting transfers between devices  19 us (33%)
  waiting for transfers between devices  4.28 us (7%)
  between operations  0.99 us (2%)
    pallas_call x1, Pallas kernels, body(): call(functools.partial(steps_kernel, nt), [shape((nz, nx, ny), F32)] * 2...  10.8 us
    ppermute x4, starting transfers between devices, shifted(): return lax.ppermute(value, axis, pairs)  10.2 us
    pallas_call x1, Pallas kernels, body(): call(functools.partial(sources_kernel, nt), state + sources, [smem_spec()...  9.81 us
    all_to_all x1, starting transfers between devices, body(): msg = lax.all_to_all(msg, AXES, split_axis=0, concat_axis=0, tiled=True)  5.12 us
    ppermute x4, waiting for transfers between devices, shifted(): return lax.ppermute(value, axis, pairs)  4.27 us
    pallas_call x1, Pallas kernels, body(): call(functools.partial(amp_kernel, (nt, ngx, ngy, nz, nx, ny)), shape((co...  3.92 us
    ppermute x3, starting transfers between devices, to_depth(): return [lax.ppermute(values[0], 'trace', [(0, 1), (1, 0)])]  3.67 us
    pallas_call x1, Pallas kernels, body(): call(columns_kernel, [shape((erows, 128), F32)] * 2, [smem_spec()] + [any...  3.67 us
  transfers between devices with their start and end apart: 8, of which 2 were waited for; matrix products, arithmetic and copies ran while one was open for 0% of the time, Pallas kernels for 35%

profile of v2, /device:TPU:10, one launch (start us, length us, event | category | flops | bytes accessed | tf_op | source)
XLA Modules:
  0.0 56.9 jit_solution(11073446723965486052)
XLA Ops:
  0.6 1.8 %shard_map.107 = (s16[8,256,256]{2,1,0:T(8,128)(2,1)S(1)}, s16[2,256,256]{2,1,0:T(8,128)(2,1)S(1)}) custom-call(s32[1]{0:T(128)} %bitcast.info_ref, f32[8,256,256]{2,1,0:T(8,128)} %now_hbm.5, f32[8,256,256]{2,1,0:T(8,128)} %prev_hbm.5, f32[8,256,256]{2,1,0:T(8,128)} %speed_hbm.5), custom_call_target="tpu_custom_call" | custom-call | bytes 3932160 | tf_op jit(solution)/shard_map/pallas_call | solution.py:725
  2.4 0.0 copy-start.1
  2.4 0.0 copy-start.2
  2.4 0.0 copy-start.3
  2.5 0.0 copy-start
  2.5 1.6 %collective-permute-start.4 = (s16[8,256,256]{2,1,0:T(8,128)(2,1)S(1)}, s16[8,256,256]{2,1,0:T(8,128)(2,1)S(1)}, u32[]{:S(2)}, u32[]{:S(2)}) collective-permute-start(s16[8,256,256]{2,1,0:T(8,128)(2,1)S(1)} %get-tuple-element.43), channel_id=1, source_target_pairs={{0,16},{16,0},{1,17},{17,1},{2,18},{18,2},{3,19},{19,3},{4,20},{20... | collective-permute-start | bytes 3145736 | tf_op jit(solution)/shard_map/ppermute | solution.py:708
  4.1 1.1 %shard_map.105 = (f32[2,8,8,256]{3,2,1,0:T(8,128)S(1)}, f32[2,8,8,256]{3,2,1,0:T(8,128)S(1)}) custom-call(f32[8,256,256]{2,1,0:T(8,128)} %now_hbm.5, f32[8,256,256]{2,1,0:T(8,128)} %prev_hbm.5, f32[8,256,256]{2,1,0:T(8,128)} %speed_hbm.5), custom_call_target="tpu_custom_call" | custom-call | bytes 1048576 | tf_op jit(solution)/shard_map/pallas_call | solution.py:735
  5.1 3.5 %collective-permute-start = (f32[2,8,8,256]{3,2,1,0:T(8,128)S(1)}, f32[2,8,8,256]{3,2,1,0:T(8,128)S(1)}, u32[]{:S(2)}, u32[]{:S(2)}) collective-permute-start(f32[2,8,8,256]{3,2,1,0:T(8,128)S(1)} %get-tuple-element.25), channel_id=1, source_target_pairs={{0,4},{4,8},{8,12},{1,5},{5,9},{9,13},{2,6},{6,10},{10,14},{3,7},{... | collective-permute-start | bytes 393224 | tf_op jit(solution)/shard_map/ppermute | solution.py:703
  8.6 2.4 %collective-permute-start.1 = (f32[2,8,8,256]{3,2,1,0:T(8,128)S(1)}, f32[2,8,8,256]{3,2,1,0:T(8,128)S(1)}, u32[]{:S(2)}, u32[]{:S(2)}) collective-permute-start(f32[2,8,8,256]{3,2,1,0:T(8,128)S(1)} %get-tuple-element.28), channel_id=1, source_target_pairs={{4,0},{8,4},{12,8},{5,1},{9,5},{13,9},{6,2},{10,6},{14,10},{7,3},{... | collective-permute-start | bytes 393224 | tf_op jit(solution)/shard_map/ppermute | solution.py:703
  11.0 0.0 copy-done.1
  11.0 0.0 copy-done.2
  11.0 0.0 copy-done.3
  11.0 0.0 copy-done
  11.1 0.1 copy.17.coupling_ref
  11.2 3.9 %shard_map.104 = f32[32,16,128]{2,1,0:T(8,128)} custom-call(bf16[256,4,256]{2,1,0:T(4,128)(2,1)} %traces_hbm.1, bf16[256,4]{1,0:T(8,128)(2,1)S(1)} %copy.17.coupling_ref, s32[3,256]{1,0:T(4,128)S(1)} %pad_add_fusion.ints_ref, f32[256,256]{1,0:T(8,128)} %constant.8.clone.table_hbm), custom_call_target="tpu_custom_call" | custom-call | flops 1073741824 | bytes 1048576 | tf_op jit(solution)/shard_map/pallas_call | solution.py:748
  15.1 0.0 collective-permute-done.top_ref
  15.1 5.1 %all-to-all-start = ((f32[32,16,128]{2,1,0:T(8,128)}), f32[32,16,128]{2,1,0:T(8,128)}, u32[]{:S(2)}, u32[]{:S(2)}) async-start(f32[32,16,128]{2,1,0:T(8,128)} %shard_map.104), calls=%async_computation | async-start | bytes 524288 | tf_op jit(solution)/shard_map/all_to_all | solution.py:764
  20.3 0.0 collective-permute-done.1.bottom_ref
  20.3 3.7 %shard_map.106 = (f32[272,128]{1,0:T(8,128)S(1)}, f32[272,128]{1,0:T(8,128)S(1)}) custom-call(s32[1]{0:T(128)} %bitcast.info_ref, f32[8,256,256]{2,1,0:T(8,128)} %now_hbm.5, f32[8,256,256]{2,1,0:T(8,128)} %prev_hbm.5, f32[8,256,256]{2,1,0:T(8,128)} %speed_hbm.5, f32[2,8,8,256]{3,2,1,0:T(8,128)S(1)} %collective-permute-done.top_ref, ...), custom_call_target="tpu_custom_call" | custom-call | bytes 6291456 | tf_op jit(solution)/shard_map/pallas_call | solution.py:767
  23.9 2.2 %collective-permute-start.3 = (f32[272,128]{1,0:T(8,128)S(1)}, f32[272,128]{1,0:T(8,128)S(1)}, u32[]{:S(2)}, u32[]{:S(2)}) collective-permute-start(f32[272,128]{1,0:T(8,128)S(1)} %get-tuple-element.29.left_ref), channel_id=1, source_target_pairs={{1,0},{2,1},{3,2},{5,4},{6,5},{7,6},{9,8},{10,9},{11,10},{13,12},{... | collective-permute-start | bytes 417800 | tf_op jit(solution)/shard_map/ppermute | solution.py:703
  26.2 2.1 %collective-permute-start.2 = (f32[272,128]{1,0:T(8,128)S(1)}, f32[272,128]{1,0:T(8,128)S(1)}, u32[]{:S(2)}, u32[]{:S(2)}) collective-permute-start(f32[272,128]{1,0:T(8,128)S(1)} %get-tuple-element.30.right_ref), channel_id=1, source_target_pairs={{0,1},{1,2},{2,3},{4,5},{5,6},{6,7},{8,9},{9,10},{10,11},{12,13},{... | collective-permute-start | bytes 417800 | tf_op jit(solution)/shard_map/ppermute | solution.py:703
  28.3 0.5 collective-permute-done.3.from_right
  28.8 3.8 %collective-permute-done.2.from_left = f32[272,128]{1,0:T(8,128)S(1)} collective-permute-done((f32[272,128]{1,0:T(8,128)S(1)}, f32[272,128]{1,0:T(8,128)S(1)}, u32[]{:S(2)}, u32[]{:S(2)}) %collective-permute-start.2) | collective-permute-done | bytes 139296 | tf_op jit(solution)/shard_map/ppermute | solution.py:703
  32.6 1.5 %collective-permute-start.5 = (s16[2,256,256]{2,1,0:T(8,128)(2,1)S(1)}, s16[2,256,256]{2,1,0:T(8,128)(2,1)S(1)}, u32[]{:S(2)}, u32[]{:S(2)}) collective-permute-start(s16[2,256,256]{2,1,0:T(8,128)(2,1)S(1)} %get-tuple-element.44), channel_id=1, source_target_pairs={{0,16},{16,0},{1,17},{17,1},{2,18},{18,2},{3,19},{19,3},{4,20},{20... | collective-permute-start | bytes 786440 | tf_op jit(solution)/shard_map/ppermute | solution.py:708
  34.0 1.4 %shard_map.108 = (f32[3,272,128]{2,1,0:T(8,128)S(1)}, s16[496,128]{1,0:T(8,128)(2,1)S(1)}) custom-call(s32[1]{0:T(128)} %bitcast.info_ref, f32[272,128]{1,0:T(8,128)S(1)} %get-tuple-element.29.left_ref, f32[272,128]{1,0:T(8,128)S(1)} %get-tuple-element.30.right_ref, f32[272,128]{1,0:T(8,128)S(1)} %collective-permute-done.2.from_left, ...), custom_call_target="tpu_custom_call" | custom-call | bytes 1048576 | tf_op jit(solution)/shard_map/pallas_call | solution.py:783
  35.4 0.6 %collective-permute-start.6 = (s16[496,128]{1,0:T(8,128)(2,1)S(1)}, s16[496,128]{1,0:T(8,128)(2,1)S(1)}, u32[]{:S(2)}, u32[]{:S(2)}) collective-permute-start(s16[496,128]{1,0:T(8,128)(2,1)S(1)} %get-tuple-element.45), channel_id=1, source_target_pairs={{0,16},{16,0},{1,17},{17,1},{2,18},{18,2},{3,19},{19,3},{4,20},{20... | collective-permute-start | bytes 380936 | tf_op jit(solution)/shard_map/ppermute | solution.py:708
  36.0 0.0 all-to-all-done.msg_hbm
  36.0 9.8 %shard_map.109 = (f32[3744,256]{1,0:T(8,128)S(1)}, f32[3744,256]{1,0:T(8,128)S(1)}, f32[3744,256]{1,0:T(8,128)S(1)}, f32[288,256]{1,0:T(8,128)S(1)}, f32[288,256...) custom-call(s32[1]{0:T(128)} %bitcast.info_ref, ...), custom_call_target="tpu_custom_call" | custom-call | flops 8388608 | bytes 8388608 | tf_op jit(solution)/shard_map/pallas_call | solution.py:800
  45.8 0.0 collective-permute-done.6.rest_10_
  45.8 0.0 collective-permute-done.5.rest_9_
  45.8 0.0 collective-permute-done.4.rest_8_
  45.9 10.8 %shard_map.110 = (f32[8,256,256]{2,1,0:T(8,128)}, f32[8,256,256]{2,1,0:T(8,128)}, f32[3744,256]{1,0:T(8,128)S(1)}, f32[3744,256]{1,0:T(8,128)S(1)}, f32[3744,256...) custom-call(s32[1]{0:T(128)} %bitcast.info_ref, ...), custom_call_target="tpu_custom_call", output_to_operand_aliasing={{2}: (1, {}), {3}: (2, {}), {4}: (3, {}), {5}: (4, {}), {6}... | custom-call | flops 33554432 | bytes 10485760 | tf_op jit(solution)/shard_map/pallas_call | solution.py:816
  (1 shorter events, 0.0 us)
Async XLA Ops:
  2.4 8.6 %copy-start.1 = (s32[256]{0:T(256)S(1)}, s32[256]{0:T(256)}, u32[]{:S(2)}) copy-start(s32[256]{0:T(256)} %param.13) | copy-start | bytes 3076
  2.4 8.6 %copy-start.2 = (s32[256,1]{0,1:T(1,128)S(1)}, s32[256,1]{0,1:T(1,128)}, u32[]{:S(2)}) copy-start(s32[256,1]{0,1:T(1,128)} %param.12) | copy-start | bytes 3076
  2.4 8.6 %copy-start.3 = (s32[256]{0:T(256)S(1)}, s32[256]{0:T(256)}, u32[]{:S(2)}) copy-start(s32[256]{0:T(256)} %param.11) | copy-start | bytes 3076
  2.5 8.6 %copy-start = (bf16[256,4]{0,1:T(4,128)(2,1)S(1)}, bf16[256,4]{0,1:T(4,128)(2,1)}, u32[]{:S(2)}) copy-start(bf16[256,4]{0,1:T(4,128)(2,1)} %param.10) | copy-start | bytes 6148
  2.5 43.4 %collective-permute-start.4 = (s16[8,256,256]{2,1,0:T(8,128)(2,1)S(1)}, s16[8,256,256]{2,1,0:T(8,128)(2,1)S(1)}, u32[]{:S(2)}, u32[]{:S(2)}) collective-permute-start(s16[8,256,256]{2,1,0:T(8,128)(2,1)S(1)} %get-tuple-element.43), channel_id=1, source_target_pairs={{0,16},{16,0},{1,17},{17,1},{2,18},{18,2},{3,19},{19,3},{4,20},{20... | collective-permute-start | bytes 3145736 | tf_op jit(solution)/shard_map/ppermute | solution.py:708
  5.1 10.0 %collective-permute-start = (f32[2,8,8,256]{3,2,1,0:T(8,128)S(1)}, f32[2,8,8,256]{3,2,1,0:T(8,128)S(1)}, u32[]{:S(2)}, u32[]{:S(2)}) collective-permute-start(f32[2,8,8,256]{3,2,1,0:T(8,128)S(1)} %get-tuple-element.25), channel_id=1, source_target_pairs={{0,4},{4,8},{8,12},{1,5},{5,9},{9,13},{2,6},{6,10},{10,14},{3,7},{... | collective-permute-start | bytes 393224 | tf_op jit(solution)/shard_map/ppermute | solution.py:703
  8.6 11.6 %collective-permute-start.1 = (f32[2,8,8,256]{3,2,1,0:T(8,128)S(1)}, f32[2,8,8,256]{3,2,1,0:T(8,128)S(1)}, u32[]{:S(2)}, u32[]{:S(2)}) collective-permute-start(f32[2,8,8,256]{3,2,1,0:T(8,128)S(1)} %get-tuple-element.28), channel_id=1, source_target_pairs={{4,0},{8,4},{12,8},{5,1},{9,5},{13,9},{6,2},{10,6},{14,10},{7,3},{... | collective-permute-start | bytes 393224 | tf_op jit(solution)/shard_map/ppermute | solution.py:703
  15.1 20.9 %all-to-all-start = ((f32[32,16,128]{2,1,0:T(8,128)}), f32[32,16,128]{2,1,0:T(8,128)}, u32[]{:S(2)}, u32[]{:S(2)}) async-start(f32[32,16,128]{2,1,0:T(8,128)} %shard_map.104), calls=%async_computation | async-start | bytes 524288 | tf_op jit(solution)/shard_map/all_to_all | solution.py:764
  23.9 4.8 %collective-permute-start.3 = (f32[272,128]{1,0:T(8,128)S(1)}, f32[272,128]{1,0:T(8,128)S(1)}, u32[]{:S(2)}, u32[]{:S(2)}) collective-permute-start(f32[272,128]{1,0:T(8,128)S(1)} %get-tuple-element.29.left_ref), channel_id=1, source_target_pairs={{1,0},{2,1},{3,2},{5,4},{6,5},{7,6},{9,8},{10,9},{11,10},{13,12},{... | collective-permute-start | bytes 417800 | tf_op jit(solution)/shard_map/ppermute | solution.py:703
  26.2 6.4 %collective-permute-start.2 = (f32[272,128]{1,0:T(8,128)S(1)}, f32[272,128]{1,0:T(8,128)S(1)}, u32[]{:S(2)}, u32[]{:S(2)}) collective-permute-start(f32[272,128]{1,0:T(8,128)S(1)} %get-tuple-element.30.right_ref), channel_id=1, source_target_pairs={{0,1},{1,2},{2,3},{4,5},{5,6},{6,7},{8,9},{9,10},{10,11},{12,13},{... | collective-permute-start | bytes 417800 | tf_op jit(solution)/shard_map/ppermute | solution.py:703
  32.6 13.3 %collective-permute-start.5 = (s16[2,256,256]{2,1,0:T(8,128)(2,1)S(1)}, s16[2,256,256]{2,1,0:T(8,128)(2,1)S(1)}, u32[]{:S(2)}, u32[]{:S(2)}) collective-permute-start(s16[2,256,256]{2,1,0:T(8,128)(2,1)S(1)} %get-tuple-element.44), channel_id=1, source_target_pairs={{0,16},{16,0},{1,17},{17,1},{2,18},{18,2},{3,19},{19,3},{4,20},{20... | collective-permute-start | bytes 786440 | tf_op jit(solution)/shard_map/ppermute | solution.py:708
  35.4 10.4 %collective-permute-start.6 = (s16[496,128]{1,0:T(8,128)(2,1)S(1)}, s16[496,128]{1,0:T(8,128)(2,1)S(1)}, u32[]{:S(2)}, u32[]{:S(2)}) collective-permute-start(s16[496,128]{1,0:T(8,128)(2,1)S(1)} %get-tuple-element.45), channel_id=1, source_target_pairs={{0,16},{16,0},{1,17},{17,1},{2,18},{18,2},{3,19},{19,3},{4,20},{20... | collective-permute-start | bytes 380936 | tf_op jit(solution)/shard_map/ppermute | solution.py:708
